TPU v7x, 256 devices: a whole 4x4x8 slice. The times are simulated.
256 devices in a mesh: dp: 8 (over z), fsdp: 32 (over y, x, core).
Axes of the slice: x: 4, y: 4, z: 8, core: 2. Of those that a mesh axis runs over, the one named last changes fastest.
Arguments:
- tokens: bfloat16 [65536, 8192], P(('dp', 'fsdp')), may hold values from -17 to 17
- output_gradient: bfloat16 [65536, 1024], P(('dp', 'fsdp')), may hold values from -17 to 17
- base_weight: bfloat16 [8192, 1024], P('fsdp'), may hold values from -0.0625 to 0.0625
- down_matrices: bfloat16 [8192, 128], replicated, may hold values from -0.0625 to 0.0625
- up_matrices: bfloat16 [1024, 128], replicated, may hold values from -0.1875 to 0.1875
- master_a: float32 [8192, 128], P(('dp', 'fsdp')), may hold values from -0.0625 to 0.0625
- moment_a: float32 [8192, 128], P(('dp', 'fsdp')), may hold values from -0.6 to 0.6
- second_a: float32 [8192, 128], P(('dp', 'fsdp')), may hold values from 0.5 to 2
- master_b: float32 [1024, 128], P(('dp', 'fsdp')), may hold values from -0.1875 to 0.1875
- moment_b: float32 [1024, 128], P(('dp', 'fsdp')), may hold values from -0.6 to 0.6
- second_b: float32 [1024, 128], P(('dp', 'fsdp')), may hold values from 0.5 to 2
- seg_counts: int32 [256, 8], P(('dp', 'fsdp')), may hold values from 1 to 128, 256 in all within a row
- bad_flags: int32 [256, 8], P(('dp', 'fsdp')), may hold values from 0 to 1, as said below
Outputs:
- input_gradient: bfloat16 [65536, 8192], P(('dp', 'fsdp'))
- new_master_a: float32 [8192, 128], P(('dp', 'fsdp'))
- new_moment_a: float32 [8192, 128], P(('dp', 'fsdp'))
- new_second_a: float32 [8192, 128], P(('dp', 'fsdp'))
- new_master_b: float32 [1024, 128], P(('dp', 'fsdp'))
- new_moment_b: float32 [1024, 128], P(('dp', 'fsdp'))
- new_second_b: float32 [1024, 128], P(('dp', 'fsdp'))
Inputs may be any that keep to these rules, and one draw needn't show every extreme that they name: `seg_counts`: each device's row sums to 256, and its largest entry is exactly 128. `bad_flags`: exactly 8 // 2 adapters are flagged, each by exactly one device.
All inputs are finite; a program needn't handle non-finite values.
Results may differ from a plain program's by a relative error of at most 0.002.
Values may be sent and summed in bfloat16 or wider, within the bound.
No kernel may reach another device: no remote copies, remote signals or barrier semaphores. Data moves between devices by JAX's collectives and lax.ppermute only.
A program may use at most 128 MiB of HBM per device.

v0:
```python
import jax
import jax.numpy as jnp
from jax import lax
from jax.sharding import PartitionSpec as P

ADAPTER_SCALE = 2.0
BETA_ONE = 0.9
BETA_TWO = 0.95
LEARN_RATE = 0.002
ADAM_EPS = 1e-08


def adam_commit(master, moment, second, grads, col_clip, col_held):
    clipped = grads * col_clip[None, :]
    new_moment = BETA_ONE * moment + (1.0 - BETA_ONE) * clipped
    new_second = BETA_TWO * second + (1.0 - BETA_TWO) * clipped * clipped
    new_master = master - LEARN_RATE * new_moment / (jnp.sqrt(new_second) + ADAM_EPS)
    keep = col_held[None, :] > 0
    return (
        jnp.where(keep, master, new_master),
        jnp.where(keep, moment, new_moment),
        jnp.where(keep, second, new_second),
    )


def shards(
    tokens,
    output_gradient,
    base_weight,
    down_matrices,
    up_matrices,
    master_a,
    moment_a,
    second_a,
    master_b,
    moment_b,
    second_b,
    seg_counts,
    bad_flags,
):
    row_count = tokens.shape[0]
    width = tokens.shape[1]
    kv_width = output_gradient.shape[1]
    col_count = down_matrices.shape[1]
    adapter_count = seg_counts.shape[1]
    adapter_rank = col_count // adapter_count
    seg_ends = jnp.cumsum(seg_counts[0])
    row_ids = jnp.arange(row_count, dtype=jnp.int32)
    row_owner = jnp.sum((row_ids[:, None] >= seg_ends[None, :]).astype(jnp.int32), axis=1)
    col_owner = jnp.arange(col_count, dtype=jnp.int32) // adapter_rank
    ownership_mask = (row_owner[:, None] == col_owner[None, :]).astype(jnp.float32)
    lowrank_product = (
        ADAPTER_SCALE
        * jnp.dot(tokens, down_matrices, preferred_element_type=jnp.float32)
        * ownership_mask
    ).astype(jnp.bfloat16)
    backward_product = (
        ADAPTER_SCALE
        * jnp.dot(output_gradient, up_matrices, preferred_element_type=jnp.float32)
        * ownership_mask
    ).astype(jnp.bfloat16)
    contract_last = (((1,), (1,)), ((), ()))
    contract_first = (((0,), (0,)), ((), ()))
    frozen_gradient = lax.dot_general(
        output_gradient,
        lax.all_gather(base_weight, "fsdp", axis=0, tiled=True),
        contract_last,
        preferred_element_type=jnp.float32,
    )
    adapter_gradient = lax.dot_general(
        backward_product, down_matrices, contract_last, preferred_element_type=jnp.float32
    )
    input_gradient = (frozen_gradient + adapter_gradient).astype(jnp.bfloat16)
    grad_a = lax.dot_general(
        tokens, backward_product, contract_first, preferred_element_type=jnp.float32
    )
    grad_b = lax.dot_general(
        output_gradient, lowrank_product, contract_first, preferred_element_type=jnp.float32
    )
    shard_a, shard_b = (
        lax.psum_scatter(grad_a, ("dp", "fsdp"), scatter_dimension=0, tiled=True),
        lax.psum_scatter(grad_b, ("dp", "fsdp"), scatter_dimension=0, tiled=True),
    )
    col_squares = jnp.sum(shard_a * shard_a, axis=0) + jnp.sum(shard_b * shard_b, axis=0)
    local_squares = jnp.sum(col_squares.reshape(adapter_count, adapter_rank), axis=1)
    local_flags = bad_flags[0]
    sum_squares = lax.psum(local_squares, ("dp", "fsdp"))
    worst_flag = lax.pmax(local_flags, ("dp", "fsdp"))
    held_back = (worst_flag > 0).astype(jnp.int32)
    limit = jnp.sqrt(jnp.float32(adapter_rank * (width + kv_width)))
    clip = limit / jnp.maximum(jnp.sqrt(sum_squares), limit)
    col_clip = jnp.repeat(clip, adapter_rank)
    col_held = jnp.repeat(held_back, adapter_rank)
    new_a = adam_commit(master_a, moment_a, second_a, shard_a, col_clip, col_held)
    new_b = adam_commit(master_b, moment_b, second_b, shard_b, col_clip, col_held)
    return (input_gradient, new_a[0], new_a[1], new_a[2], new_b[0], new_b[1], new_b[2])


def solution(mesh):
    return jax.shard_map(
        shards,
        mesh=mesh,
        in_specs=(
            P(("dp", "fsdp"), None),
            P(("dp", "fsdp"), None),
            P("fsdp", None),
            P(),
            P(),
            P(("dp", "fsdp"), None),
            P(("dp", "fsdp"), None),
            P(("dp", "fsdp"), None),
            P(("dp", "fsdp"), None),
            P(("dp", "fsdp"), None),
            P(("dp", "fsdp"), None),
            P(("dp", "fsdp"), None),
            P(("dp", "fsdp"), None),
        ),
        out_specs=(
            P(("dp", "fsdp"), None),
            P(("dp", "fsdp"), None),
            P(("dp", "fsdp"), None),
            P(("dp", "fsdp"), None),
            P(("dp", "fsdp"), None),
            P(("dp", "fsdp"), None),
            P(("dp", "fsdp"), None),
        ),
        check_vma=False,
    )
```

profile of v0, /device:TPU:32, one launch (start us, length us, event | category | flops | bytes accessed | tf_op | source)
XLA Modules:
  0.0 1666.1 jit_solution(76637667198186911)
XLA Ops:
  8.1 1.0 reduce-window.8
  9.1 0.1 convert_reduce_fusion
  9.2 0.4 copy-done
  9.6 4.6 convolution_bitcast_fusion.1
  14.3 0.3 fusion.3
  14.6 5.0 convolution_bitcast_fusion
  19.6 5.6 copy.102
  25.3 0.5 all-gather.2.cloned.1.call-update
  25.8 80.8 %pmax.7 = s32[8]{0:T(128)S(1)} all-reduce(s32[8]{0:T(128)S(1)} %bitcast.22), channel_id=1, replica_groups=mesh['dp'=8,'fsdp'=32] {'dp','fsdp'}, use_global_device_ids=true, to_apply=%region_2.3 | all-reduce | flops 8 | bytes 64 | tf_op jit(solution)/shard_map/pmax | solution.py:88
  106.6 0.1 copy.93
  106.7 0.1 broadcast_in_dim.38
  106.8 0.1 gt.18
  106.9 0.1 copy.95
  107.0 0.1 copy.92
  107.1 172.0 %all-reduce.3.cloned.1.call-done = f32[1024,128]{0,1:T(8,128)} async-done(((f32[1024,128]{0,1:T(8,128)}), f32[1024,128]{0,1:T(8,128)}) %all-reduce.3.cloned.1.call-update) | async-done | bytes 524304
  279.1 1.0 multiply_reduce_fusion
  280.1 1174.5 %reduce-scatter.5.cloned.1.call-done = f32[32,128]{1,0:T(8,128)} async-done(((f32[8192,128]{1,0:T(8,128)}), f32[32,128]{1,0:T(8,128)}) %reduce-scatter.5.cloned.1.call-update) | async-done | bytes 16400
  1454.6 0.8 copy.103
  1455.4 0.1 multiply_reduce_fusion.1
  1455.5 0.1 add.47
  1455.6 0.1 reduce_sum.39
  1455.7 0.1 copy.98
  1455.8 174.4 %psum.7 = f32[8]{0:T(128)S(1)} all-reduce(f32[8]{0:T(128)S(1)} %reduce_sum.39), channel_id=1, replica_groups=mesh['dp'=8,'fsdp'=32] {'dp','fsdp'}, use_global_device_ids=true, to_apply=%region_8.9 | all-reduce | flops 8 | bytes 64 | tf_op jit(solution)/shard_map/psum | solution.py:87
  1630.2 0.1 broadcast_in_dim.40
  1630.2 0.1 mul.110
  1630.3 0.1 fusion.12
  1630.5 0.7 copy.99
  1631.2 0.7 copy.100
  1631.8 0.7 copy.101
  1632.5 0.6 fusion.15
  1633.1 18.8 %fusion.19 = f32[256,8192]{1,0:T(8,128)} fusion(bf16[256,1024]{1,0:T(8,128)(2,1)S(1)} %copy-done.1, bf16[8192,1024]{1,0:T(8,128)(2,1)} %all-gather.2.cloned.1.call-done), kind=kOutput, calls=%fused_computation.41 | convolution fusion | flops 4294967296 | bytes 25690112 | tf_op jit(solution)/shard_map/dot_general | solution.py:64
  1652.0 6.6 fusion
  (29 shorter events, 0.2 us)
Async XLA Ops:
  8.0 1.6 copy-start
  8.0 6.3 copy-start.1
  8.0 6.3 copy-start.8
  8.0 271.0 %all-reduce.3.cloned.1.call-start = ((), (), s32[]{:S(2)}) async-start(), calls=%async_computation.3 | async-start | bytes 1048576
  14.2 1440.4 %reduce-scatter.5.cloned.1.call-start = ((), (), s32[]{:S(2)}) async-start(), calls=%async_computation.2 | async-start | bytes 4210688
  25.1 0.7 copy-start.9
  25.1 81.5 %copy-start.2 = (f32[32,128]{1,0:T(8,128)S(1)}, f32[32,128]{1,0:T(8,128)}, u32[]{:S(2)}) copy-start(f32[32,128]{1,0:T(8,128)} %param.20) | copy-start | bytes 49156
  25.1 81.8 %copy-start.3 = (f32[32,128]{1,0:T(8,128)S(1)}, f32[32,128]{1,0:T(8,128)}, u32[]{:S(2)}) copy-start(f32[32,128]{1,0:T(8,128)} %param.18) | copy-start | bytes 49156
  25.1 81.9 %copy-start.4 = (f32[32,128]{1,0:T(8,128)S(1)}, f32[32,128]{1,0:T(8,128)}, u32[]{:S(2)}) copy-start(f32[32,128]{1,0:T(8,128)} %param.19) | copy-start | bytes 49156
  25.1 1607.4 %copy-start.5 = (f32[4,128]{1,0:T(4,128)S(1)}, f32[4,128]{1,0:T(4,128)}, u32[]{:S(2)}) copy-start(f32[4,128]{1,0:T(4,128)} %param.23) | copy-start | bytes 6148
  25.2 1607.4 %copy-start.6 = (f32[4,128]{1,0:T(4,128)S(1)}, f32[4,128]{1,0:T(4,128)}, u32[]{:S(2)}) copy-start(f32[4,128]{1,0:T(4,128)} %param.21) | copy-start | bytes 6148
  25.2 1607.3 %copy-start.7 = (f32[4,128]{1,0:T(4,128)S(1)}, f32[4,128]{1,0:T(4,128)}, u32[]{:S(2)}) copy-start(f32[4,128]{1,0:T(4,128)} %param.22) | copy-start | bytes 6148
  25.2 1607.9 %all-gather.2.cloned.1.call-start = ((), (), s32[]{:S(2)}) async-start(), calls=%async_computation.1 | async-start | bytes 17301504 | tf_op jit(solution)/shard_map/all_gather | solution.py:66
Sparse Core Ops, SparseCore 0:
  14.4 264.6 all-reduce.2
  281.6 1173.0 reduce-scatter.4
Sparse Core Ops, SparseCore 1:
  28.2 81.3 all-gather.1
where the time goes:
time: 1670 us
  waiting for transfers between devices  1350 us (81%)
  blocking collectives  255 us (15%)
  matrix products  35.3 us (2%)
    unnamed x5, waiting for transfers between devices  1350 us
    psum x1, blocking collectives, shards(): sum_squares = lax.psum(local_squares, ('dp', 'fsdp'))  174 us
    pmax x1, blocking collectives, shards(): worst_flag = lax.pmax(local_flags, ('dp', 'fsdp'))  80.8 us
  transfers between devices with their start and end apart: 3, of which 2 were waited for; matrix products, arithmetic and copies ran while one was open for 1% of the time, Pallas kernels for 0%

commit v1 on v0

v1 whole, which is shorter than its diff:
```python
import functools

import jax
import jax.numpy as jnp
from jax import lax
from jax.experimental import pallas as pl
from jax.experimental.pallas import tpu as pltpu
from jax.sharding import Mesh
from jax.sharding import PartitionSpec as P

ADAPTER_SCALE = 2.0
BETA_ONE = 0.9
BETA_TWO = 0.95
LEARN_RATE = 0.002
ADAM_EPS = 1e-08

DEV = ("z", "y", "x", "c")
PLANE = ("y", "x", "c")
F32 = jnp.float32
BF16 = jnp.bfloat16
CONTRACT_LAST = (((1,), (1,)), ((), ()))
CONTRACT_FIRST = (((0,), (0,)), ((), ()))

VMEM = pl.BlockSpec(memory_space=pltpu.VMEM)
SMEM = pl.BlockSpec(memory_space=pltpu.SMEM)
HBM = pl.BlockSpec(memory_space=pl.ANY)


def call(kernel, outs, ins, scratch=(), limit=48, flops=0, nbytes=0):
    return pl.pallas_call(
        kernel,
        out_shape=outs,
        in_specs=ins,
        out_specs=jax.tree.map(lambda _: VMEM, outs),
        scratch_shapes=list(scratch),
        compiler_params=pltpu.CompilerParams(vmem_limit_bytes=limit << 20),
        cost_estimate=pl.CostEstimate(flops=flops, bytes_accessed=nbytes, transcendentals=0),
    )


def grads_kernel(
    where_ref, counts_ref, tok_hbm, g_hbm, down_hbm, up_hbm,
    keep_ref, send_ref, back_ref,
    tok, g, down, up, sems, small_sems,
):
    rows, width = tok.shape
    kv = g.shape[1]
    cols = down.shape[1]
    adapters = counts_ref.shape[1]
    rank = cols // adapters
    tiles = sems.shape[0]
    tile = width // tiles
    blocks = keep_ref.shape[0]
    block = width // blocks
    kv_block = kv // blocks
    half = block // 8
    mine = where_ref[3]

    g_copy = pltpu.make_async_copy(g_hbm, g, small_sems.at[0])
    up_copy = pltpu.make_async_copy(up_hbm, up, small_sems.at[1])
    g_copy.start()
    up_copy.start()
    tok_copies = []
    for t in range(tiles):
        span = pl.ds(t * tile, tile)
        a = pltpu.make_async_copy(tok_hbm.at[:, span], tok.at[:, span], sems.at[t, 0])
        b = pltpu.make_async_copy(down_hbm.at[span, :], down.at[span, :], sems.at[t, 1])
        a.start()
        b.start()
        tok_copies.append((a, b))

    row_ids = lax.broadcasted_iota(jnp.int32, (rows, cols), 0)
    col_owner = lax.broadcasted_iota(jnp.int32, (rows, cols), 1) // rank
    owner = jnp.zeros((rows, cols), jnp.int32)
    end = jnp.int32(0)
    for e in range(adapters):
        end = end + counts_ref[0, e]
        owner = owner + (row_ids >= end).astype(jnp.int32)
    mask = (owner == col_owner).astype(F32)

    g_copy.wait()
    up_copy.wait()
    back = (
        ADAPTER_SCALE * jnp.dot(g[...], up[...], preferred_element_type=F32) * mask
    ).astype(BF16)
    back_ref[...] = back

    acc = jnp.zeros((rows, cols), F32)
    for t in range(tiles):
        tok_copies[t][0].wait()
        tok_copies[t][1].wait()
        span = slice(t * tile, (t + 1) * tile)
        acc = acc + jnp.dot(tok[:, span], down[span, :], preferred_element_type=F32)
        for s in range(tile // block):
            b = t * (tile // block) + s
            r = lax.dot_general(
                tok[:, b * block : (b + 1) * block], back, CONTRACT_FIRST,
                preferred_element_type=F32,
            ).reshape(4, 2, half, cols)
            first = mine == 0
            keep_ref[b, : 4 * half] = jnp.where(first, r[:, 0], r[:, 1]).reshape(4 * half, cols)
            send_ref[b, : 4 * half] = jnp.where(first, r[:, 1], r[:, 0]).reshape(4 * half, cols)
    low = (ADAPTER_SCALE * acc * mask).astype(BF16)
    group = 256 // kv_block
    for s in range(kv // 256):
        r = lax.dot_general(
            g[:, s * 256 : (s + 1) * 256], low, CONTRACT_FIRST, preferred_element_type=F32
        ).reshape(group, kv_block, cols)
        keep_ref[s * group : (s + 1) * group, 4 * half :] = r
        send_ref[s * group : (s + 1) * group, 4 * half :] = r


def to_z_kernel(where_ref, keep_ref, recv_ref, *outs):
    count = len(outs)
    me = where_ref[0]
    per = keep_ref.shape[0] // count
    for k in range(count):
        to = lax.rem(me + k, count) * per
        for j in range(per):
            rows = keep_ref.shape[1]
            total = keep_ref[to + j] + recv_ref[to + j]
            outs[k][j * rows : (j + 1) * rows] = total.astype(outs[k].dtype)


def to_y_kernel(where_ref, *refs):
    ins, outs = refs[:-4], refs[-4:]
    me = where_ref[1]
    rows = outs[0].shape[0]
    for k in range(4):
        span = pl.ds(pl.multiple_of(lax.rem(me + k, 4) * rows, rows), rows)
        total = ins[0][span]
        for r in ins[1:]:
            total = total + r[span].astype(F32)
        outs[k][...] = total


def to_x_kernel(flags_ref, a, b, c, d, out):
    rows = a.shape[0]
    cols = a.shape[1]
    adapters = flags_ref.shape[1]
    rank = cols // adapters
    out[:rows] = (a[...] + b[...]) + (c[...] + d[...])
    owner = lax.broadcasted_iota(jnp.int32, (8, cols), 1) // rank
    flags = jnp.zeros((8, cols), F32)
    for e in range(adapters):
        flags = jnp.where(owner == e, flags_ref[0, e].astype(F32), flags)
    out[rows:] = flags


def squares_kernel(where_ref, a, b, c, d, total_ref, squares_ref):
    rows = total_ref.shape[0]
    cols = total_ref.shape[1]
    wide = rows * 4 // 5
    total = (a[...] + b[...]) + (c[...] + d[...])
    total_ref[...] = total[:rows]
    part_a = total[:wide]
    part_b = total[wide:rows]
    owner = (lax.broadcasted_iota(jnp.int32, part_b.shape, 0) // 4) % 2
    part_b = jnp.where(owner == where_ref[3], part_b, 0.0)
    squares = jnp.sum(part_a * part_a, axis=0, keepdims=True) + jnp.sum(
        part_b * part_b, axis=0, keepdims=True
    )
    row = lax.broadcasted_iota(jnp.int32, (8, cols), 0)
    squares_ref[...] = jnp.where(row == 0, squares, total[rows:])


def adam_kernel(
    limit_sq, where_ref, total_ref, squares_ref,
    master_a, moment_a, second_a, master_b, moment_b, second_b,
    out_ma, out_oa, out_sa, out_mb, out_ob, out_sb,
):
    rows, cols = master_a.shape
    adapters = 8
    rank = cols // adapters
    col_squares = squares_ref[0:1]
    flags = squares_ref[1:2]
    owner = lax.broadcasted_iota(jnp.int32, (1, cols), 1) // rank
    sums = jnp.zeros((1, cols), F32)
    for e in range(adapters):
        one = jnp.sum(jnp.where(owner == e, col_squares, 0.0), axis=1, keepdims=True)
        sums = jnp.where(owner == e, one, sums)
    limit = jnp.sqrt(jnp.full((1, cols), limit_sq, F32))
    clip = limit / jnp.maximum(jnp.sqrt(sums), limit)
    held = flags > 0.5

    def commit(grad, master, moment, second, to_master, to_moment, to_second):
        clipped = grad * clip
        m, o, s = master[...], moment[...], second[...]
        new_o = BETA_ONE * o + (1.0 - BETA_ONE) * clipped
        new_s = BETA_TWO * s + (1.0 - BETA_TWO) * clipped * clipped
        new_m = m - LEARN_RATE * new_o / (jnp.sqrt(new_s) + ADAM_EPS)
        to_master[...] = jnp.where(held, m, new_m)
        to_moment[...] = jnp.where(held, o, new_o)
        to_second[...] = jnp.where(held, s, new_s)

    x = where_ref[2]
    grad_a = total_ref[pl.ds(pl.multiple_of(x * rows, rows), rows)]
    pair = total_ref[pl.ds(pl.multiple_of(4 * rows + x * 8, 8), 8)]
    grad_b = jnp.where(where_ref[3] == 0, pair[:4], pair[4:])
    commit(grad_a, master_a, moment_a, second_a, out_ma, out_oa, out_sa)
    commit(grad_b, master_b, moment_b, second_b, out_mb, out_ob, out_sb)


def input_grad_kernel(g, weight, back, down, out):
    total = lax.dot_general(g[...], weight[...], CONTRACT_LAST, preferred_element_type=F32)
    total = total + lax.dot_general(
        back[...], down[...], CONTRACT_LAST, preferred_element_type=F32
    )
    out[...] = total.astype(out.dtype)


def input_grad(g, weight, back, down, tile):
    rows, kv = g.shape
    width, cols = down.shape
    return pl.pallas_call(
        input_grad_kernel,
        grid=(width // tile,),
        out_shape=jax.ShapeDtypeStruct((rows, width), BF16),
        in_specs=[
            pl.BlockSpec((rows, kv), lambda i: (0, 0)),
            pl.BlockSpec((tile, kv), lambda i: (i, 0)),
            pl.BlockSpec((rows, cols), lambda i: (0, 0)),
            pl.BlockSpec((tile, cols), lambda i: (i, 0)),
        ],
        out_specs=pl.BlockSpec((rows, tile), lambda i: (0, i)),
        compiler_params=pltpu.CompilerParams(vmem_limit_bytes=32 << 20),
        cost_estimate=pl.CostEstimate(
            flops=2 * rows * width * (kv + cols),
            bytes_accessed=2 * width * (kv + cols + rows),
            transcendentals=0,
        ),
    )(g, weight, back, down)


def shift(value, axis, size, by):
    return lax.ppermute(value, axis, [(i, (i + by) % size) for i in range(size)])


def flip(value, axis, size, bit):
    return lax.ppermute(value, axis, [(i, i ^ bit) for i in range(size)])


def shards(sizes, tokens, g, base_weight, down, up, ma, oa, sa, mb, ob, sb, counts, flags):
    nz, ny, nx, nc = sizes
    rows, width = tokens.shape
    kv = g.shape[1]
    cols = down.shape[1]
    where = jnp.stack([lax.axis_index(a) for a in DEV]).astype(jnp.int32)
    sds = jax.ShapeDtypeStruct

    weight = lax.all_gather(base_weight, PLANE, axis=0, tiled=True)

    blocks = nz * ny
    deep = width // blocks // nc + kv // blocks
    part = sds((blocks, deep, cols), F32)
    tiles = 8
    keep, send, back = call(
        grads_kernel,
        (part, part, sds((rows, cols), BF16)),
        [SMEM, SMEM, HBM, HBM, HBM, HBM],
        [
            pltpu.VMEM((rows, width), BF16),
            pltpu.VMEM((rows, kv), BF16),
            pltpu.VMEM((width, cols), BF16),
            pltpu.VMEM((kv, cols), BF16),
            pltpu.SemaphoreType.DMA((tiles, 2)),
            pltpu.SemaphoreType.DMA((2,)),
        ],
        flops=4 * rows * width * cols,
        nbytes=12 << 20,
    )(where, counts, tokens, g, down, up)

    recv = flip(send, "c", nc, 1)
    z_rows = ny * deep
    out_z = tuple(sds((z_rows, cols), F32 if k == 0 else BF16) for k in range(nz))
    to_z = call(to_z_kernel, out_z, [SMEM, VMEM, VMEM], nbytes=6 << 20)(where, keep, recv)
    from_z = [to_z[0]] + [shift(to_z[k], "z", nz, k) for k in range(1, nz)]
    out_y = tuple(sds((deep, cols), F32) for _ in range(ny))
    to_y = call(to_y_kernel, out_y, [SMEM] + [VMEM] * nz, nbytes=2 << 20)(where, *from_z)
    from_y = [to_y[0]] + [shift(to_y[k], "y", ny, k) for k in range(1, ny)]
    to_x = call(to_x_kernel, sds((deep + 8, cols), F32), [SMEM] + [VMEM] * ny)(flags, *from_y)
    from_x = [to_x] + [shift(to_x, "x", nx, k) for k in range(1, nx)]
    total, squares = call(
        squares_kernel, (sds((deep, cols), F32), sds((8, cols), F32)), [SMEM] + [VMEM] * nx
    )(where, *from_x)
    for axis, size in (("c", nc), ("y", ny), ("z", nz)):
        bit = 1
        while bit < size:
            squares = squares + flip(squares, axis, size, bit)
            bit *= 2

    shape = lambda v: sds(v.shape, v.dtype)
    new = call(
        functools.partial(adam_kernel, float(cols // 8 * (width + kv))),
        tuple(shape(v) for v in (ma, oa, sa, mb, ob, sb)),
        [SMEM] + [VMEM] * 8,
    )(where, total, squares, ma, oa, sa, mb, ob, sb)
    out = input_grad(g, weight, back, down, 512)
    return (out, *new)


def solution(mesh):
    sizes = (8, 4, 4, 2)
    fine = Mesh(mesh.devices.reshape(sizes), DEV)
    split = P(DEV, None)
    return jax.shard_map(
        functools.partial(shards, sizes),
        mesh=fine,
        in_specs=(split, split, P(PLANE, None), P(), P()) + (split,) * 8,
        out_specs=(split,) * 7,
        check_vma=False,
    )
```

time: 1670 us -> 144 us (0.09)
  waiting for transfers between devices: 1350 us -> 57.4 us
  blocking collectives: 255 us -> 0 us
  starting transfers between devices: 0.12 us -> 37.6 us
  matrix products: 35.3 us -> 0 us
  Pallas kernels: 0 us -> 22.8 us
    unnamed x5 -> x1, waiting for transfers between devices: 1350 us -> 0.68 us
    psum x1 -> x0, blocking collectives: 174 us -> none  [shards(): sum_squares = lax.psum(local_squares, ('dp', 'fsdp'))]
    pmax x1 -> x0, blocking collectives: 80.8 us -> none  [shards(): worst_flag = lax.pmax(local_flags, ('dp', 'fsdp'))]
    ppermute x0 -> x20, waiting for transfers between devices: none -> 56.7 us  [the longest x13 34.4 us: shift(): lax.ppermute(value, axis, [(i, (i + by) % size) for i in range(size)])]
    ppermute x0 -> x20, starting transfers between devices: none -> 37.6 us  [the longest x13 29.1 us: shift(): lax.ppermute(value, axis, [(i, (i + by) % size) for i in range(size)])]
    dot_general x5 -> x0, matrix products: 35.3 us -> none  [the longest x1 18.8 us: shards(): lax.dot_general(output_gradient, lax.all_gather(base_weight, 'fsdp', axis...]
    pallas_call x0 -> x7, Pallas kernels: none -> 22.8 us  [the longest x1 10.2 us: input_grad(): pl.pallas_call(input_grad_kernel, grid=(width // tile,), out_shape=jax.Sh...]
  transfers between devices with their start and end apart: 3 -> 21, of which waited for: 2 -> 17; matrix products, arithmetic and copies ran while one was open for 1% -> 0% of each run, Pallas kernels for 0% -> 9%
where the time goes in v1:
time: 144 us
  waiting for transfers between devices  57.4 us (40%)
  starting transfers between devices  37.6 us (26%)
  Pallas kernels  22.8 us (16%)
  between operations  14.2 us (10%)
  local copies, waits for them, and re-layouts  11.5 us (8%)
    ppermute x13, waiting for transfers between devices, shift(): lax.ppermute(value, axis, [(i, (i + by) % size) for i in range(size)])  34.4 us
    ppermute x13, starting transfers between devices, shift(): lax.ppermute(value, axis, [(i, (i + by) % size) for i in range(size)])  29.1 us
    ppermute x7, waiting for transfers between devices, flip(): return lax.ppermute(value, axis, [(i, i ^ bit) for i in range(size)])  22.3 us
    unnamed x30, local copies, waits for them, and re-layouts  11.5 us
    pallas_call x1, Pallas kernels, input_grad(): pl.pallas_call(input_grad_kernel, grid=(width // tile,), out_shape=jax.Sh...  10.2 us
    ppermute x7, starting transfers between devices, flip(): return lax.ppermute(value, axis, [(i, i ^ bit) for i in range(size)])  8.47 us
    pallas_call x1, Pallas kernels, shards(): call(grads_kernel, (part, part, sds((rows, cols), BF16)), [SMEM, SMEM, HB...  6.97 us
  transfers between devices with their start and end apart: 21, of which 17 were waited for; matrix products, arithmetic and copies ran while one was open for 0% of the time, Pallas kernels for 9%

profile of v1, /device:TPU:32, one launch (start us, length us, event | category | flops | bytes accessed | tf_op | source)
XLA Modules:
  0.0 143.6 jit_solution(3604511493926649567)
XLA Ops:
  8.0 1.6 %copy-done.1 = bf16[8192,128]{1,0:T(8,128)(2,1)S(1)} copy-done((bf16[8192,128]{1,0:T(8,128)(2,1)S(1)}, bf16[8192,128]{1,0:T(8,128)(2,1)}, u32[]{:S(2)}) %copy-start.1) | copy-done | bytes 2097176
  12.2 7.0 %shard_map.180 = (f32[32,160,128]{2,1,0:T(8,128)S(1)}, f32[32,160,128]{2,1,0:T(8,128)}, bf16[256,128]{1,0:T(8,128)(2,1)S(1)}) custom-call(s32[4]{0:T(128)S(1)} %pad_add_fusion.where_ref, s32[1,8]{1,0:T(1,128)S(1)} %copy-done.13, bf16[256,8192]{1,0:T(8,128)(2,1)} %tok_hbm.1, bf16[256,1024]{1,0:T(8,128)(2,1)S(1)} %copy-done.3, ...), custom_call_target="tpu_custom_call" | custom-call | flops 1073741824 | bytes 12582912 | tf_op jit(solution)/shard_map/pallas_call | solution.py:257
  19.3 5.1 %collective-permute-done.recv_ref = f32[32,160,128]{2,1,0:T(8,128)S(1)} collective-permute-done((f32[32,160,128]{2,1,0:T(8,128)}, f32[32,160,128]{2,1,0:T(8,128)S(1)}, u32[]{:S(2)}, u32[]{:S(2)}) %collective-permute-start) | collective-permute-done | bytes 2621472 | tf_op jit(solution)/shard_map/ppermute | solution.py:240
  24.4 1.5 %copy-done.14 = f32[32,160,128]{2,1,0:T(8,128)} copy-done((f32[32,160,128]{2,1,0:T(8,128)}, f32[32,160,128]{2,1,0:T(8,128)S(1)}, u32[]{:S(2)}) %copy-start.14) | copy-done | bytes 2621464
  26.0 2.5 %shard_map.182 = (f32[640,128]{1,0:T(8,128)S(1)}, bf16[640,128]{1,0:T(8,128)(2,1)S(1)}, bf16[640,128]{1,0:T(8,128)(2,1)S(1)}, bf16[640,128]{1,0:T(8,128)(2,1)S(1...) custom-call(s32[4]{0:T(128)S(1)} %pad_add_fusion.where_ref, ...), custom_call_target="tpu_custom_call" | custom-call | bytes 6291456 | tf_op jit(solution)/shard_map/pallas_call | solution.py:276
  28.5 2.0 %collective-permute-start.1 = (bf16[640,128]{1,0:T(8,128)(2,1)S(1)}, bf16[640,128]{1,0:T(8,128)(2,1)S(1)}, u32[]{:S(2)}, u32[]{:S(2)}) collective-permute-start(bf16[640,128]{1,0:T(8,128)(2,1)S(1)} %get-tuple-element.34), channel_id=1, source_target_pairs={{0,32},{32,64},{64,96},{96,128},{128,160},{160,192},{192,224},{224... | collective-permute-start | bytes 491528 | tf_op jit(solution)/shard_map/ppermute | solution.py:236
  30.4 4.3 %collective-permute-start.2 = (bf16[640,128]{1,0:T(8,128)(2,1)S(1)}, bf16[640,128]{1,0:T(8,128)(2,1)S(1)}, u32[]{:S(2)}, u32[]{:S(2)}) collective-permute-start(bf16[640,128]{1,0:T(8,128)(2,1)S(1)} %get-tuple-element.35), channel_id=1, source_target_pairs={{0,64},{32,96},{64,128},{96,160},{128,192},{160,224},{192,0},{224,... | collective-permute-start | bytes 491528 | tf_op jit(solution)/shard_map/ppermute | solution.py:236
  34.8 1.9 %collective-permute-start.3 = (bf16[640,128]{1,0:T(8,128)(2,1)S(1)}, bf16[640,128]{1,0:T(8,128)(2,1)S(1)}, u32[]{:S(2)}, u32[]{:S(2)}) collective-permute-start(bf16[640,128]{1,0:T(8,128)(2,1)S(1)} %get-tuple-element.36), channel_id=1, source_target_pairs={{0,96},{32,128},{64,160},{96,192},{128,224},{160,0},{192,32},{224,... | collective-permute-start | bytes 491528 | tf_op jit(solution)/shard_map/ppermute | solution.py:236
  36.7 1.5 %collective-permute-start.4 = (bf16[640,128]{1,0:T(8,128)(2,1)S(1)}, bf16[640,128]{1,0:T(8,128)(2,1)S(1)}, u32[]{:S(2)}, u32[]{:S(2)}) collective-permute-start(bf16[640,128]{1,0:T(8,128)(2,1)S(1)} %get-tuple-element.37), channel_id=1, source_target_pairs={{0,128},{32,160},{64,192},{96,224},{128,0},{160,32},{192,64},{224,... | collective-permute-start | bytes 491528 | tf_op jit(solution)/shard_map/ppermute | solution.py:236
  38.2 3.1 %collective-permute-start.5 = (bf16[640,128]{1,0:T(8,128)(2,1)S(1)}, bf16[640,128]{1,0:T(8,128)(2,1)S(1)}, u32[]{:S(2)}, u32[]{:S(2)}) collective-permute-start(bf16[640,128]{1,0:T(8,128)(2,1)S(1)} %get-tuple-element.38), channel_id=1, source_target_pairs={{0,160},{32,192},{64,224},{96,0},{128,32},{160,64},{192,96},{224,1... | collective-permute-start | bytes 491528 | tf_op jit(solution)/shard_map/ppermute | solution.py:236
  41.3 2.4 %collective-permute-start.6 = (bf16[640,128]{1,0:T(8,128)(2,1)S(1)}, bf16[640,128]{1,0:T(8,128)(2,1)S(1)}, u32[]{:S(2)}, u32[]{:S(2)}) collective-permute-start(bf16[640,128]{1,0:T(8,128)(2,1)S(1)} %get-tuple-element.39), channel_id=1, source_target_pairs={{0,192},{32,224},{64,0},{96,32},{128,64},{160,96},{192,128},{224,1... | collective-permute-start | bytes 491528 | tf_op jit(solution)/shard_map/ppermute | solution.py:236
  43.7 2.6 %collective-permute-done.2.refs_2_ = bf16[640,128]{1,0:T(8,128)(2,1)S(1)} collective-permute-done((bf16[640,128]{1,0:T(8,128)(2,1)S(1)}, bf16[640,128]{1,0:T(8,128)(2,1)S(1)}, u32[]{:S(2)}, u32[]{:S(2)}) %collective-permute-start.2) | collective-permute-done | bytes 163872 | tf_op jit(solution)/shard_map/ppermute | solution.py:236
  46.2 2.9 %collective-permute-start.7 = (bf16[640,128]{1,0:T(8,128)(2,1)S(1)}, bf16[640,128]{1,0:T(8,128)(2,1)S(1)}, u32[]{:S(2)}, u32[]{:S(2)}) collective-permute-start(bf16[640,128]{1,0:T(8,128)(2,1)S(1)} %get-tuple-element.40), channel_id=1, source_target_pairs={{0,224},{32,0},{64,32},{96,64},{128,96},{160,128},{192,160},{224,1... | collective-permute-start | bytes 491528 | tf_op jit(solution)/shard_map/ppermute | solution.py:236
  49.1 12.2 %collective-permute-done.3.refs_3_ = bf16[640,128]{1,0:T(8,128)(2,1)S(1)} collective-permute-done((bf16[640,128]{1,0:T(8,128)(2,1)S(1)}, bf16[640,128]{1,0:T(8,128)(2,1)S(1)}, u32[]{:S(2)}, u32[]{:S(2)}) %collective-permute-start.3) | collective-permute-done | bytes 163872 | tf_op jit(solution)/shard_map/ppermute | solution.py:236
  61.3 6.5 %collective-permute-done.6.refs_6_ = bf16[640,128]{1,0:T(8,128)(2,1)S(1)} collective-permute-done((bf16[640,128]{1,0:T(8,128)(2,1)S(1)}, bf16[640,128]{1,0:T(8,128)(2,1)S(1)}, u32[]{:S(2)}, u32[]{:S(2)}) %collective-permute-start.6) | collective-permute-done | bytes 163872 | tf_op jit(solution)/shard_map/ppermute | solution.py:236
  67.8 1.9 %collective-permute-done.7.refs_7_ = bf16[640,128]{1,0:T(8,128)(2,1)S(1)} collective-permute-done((bf16[640,128]{1,0:T(8,128)(2,1)S(1)}, bf16[640,128]{1,0:T(8,128)(2,1)S(1)}, u32[]{:S(2)}, u32[]{:S(2)}) %collective-permute-start.7) | collective-permute-done | bytes 163872 | tf_op jit(solution)/shard_map/ppermute | solution.py:236
  70.5 3.1 %collective-permute-start.10 = (f32[160,128]{1,0:T(8,128)S(1)}, f32[160,128]{1,0:T(8,128)S(1)}, u32[]{:S(2)}, u32[]{:S(2)}) collective-permute-start(f32[160,128]{1,0:T(8,128)S(1)} %get-tuple-element.44), channel_id=1, source_target_pairs={{0,24},{8,0},{16,8},{24,16},{1,25},{9,1},{17,9},{25,17},{2,26},{10... | collective-permute-start | bytes 245768 | tf_op jit(solution)/shard_map/ppermute | solution.py:236
  73.5 2.2 %collective-permute-start.9 = (f32[160,128]{1,0:T(8,128)S(1)}, f32[160,128]{1,0:T(8,128)S(1)}, u32[]{:S(2)}, u32[]{:S(2)}) collective-permute-start(f32[160,128]{1,0:T(8,128)S(1)} %get-tuple-element.43), channel_id=1, source_target_pairs={{0,16},{8,24},{16,0},{24,8},{1,17},{9,25},{17,1},{25,9},{2,18},{10... | collective-permute-start | bytes 245768 | tf_op jit(solution)/shard_map/ppermute | solution.py:236
  75.7 2.0 %collective-permute-done.10.d = f32[160,128]{1,0:T(8,128)S(1)} collective-permute-done((f32[160,128]{1,0:T(8,128)S(1)}, f32[160,128]{1,0:T(8,128)S(1)}, u32[]{:S(2)}, u32[]{:S(2)}) %collective-permute-start.10) | collective-permute-done | bytes 81952 | tf_op jit(solution)/shard_map/ppermute | solution.py:236
  77.8 5.0 %collective-permute-done.8.b = f32[160,128]{1,0:T(8,128)S(1)} collective-permute-done((f32[160,128]{1,0:T(8,128)S(1)}, f32[160,128]{1,0:T(8,128)S(1)}, u32[]{:S(2)}, u32[]{:S(2)}) %collective-permute-start.8) | collective-permute-done | bytes 81952 | tf_op jit(solution)/shard_map/ppermute | solution.py:236
  84.5 1.6 %collective-permute-start.11 = (f32[168,128]{1,0:T(8,128)S(1)}, f32[168,128]{1,0:T(8,128)S(1)}, u32[]{:S(2)}, u32[]{:S(2)}) collective-permute-start(f32[168,128]{1,0:T(8,128)S(1)} %shard_map.184.a), channel_id=1, source_target_pairs={{0,2},{2,4},{4,6},{6,0},{1,3},{3,5},{5,7},{7,1},{8,10},{10,12},{12... | collective-permute-start | bytes 258056 | tf_op jit(solution)/shard_map/ppermute | solution.py:236
  86.0 2.8 %collective-permute-start.12 = (f32[168,128]{1,0:T(8,128)S(1)}, f32[168,128]{1,0:T(8,128)S(1)}, u32[]{:S(2)}, u32[]{:S(2)}) collective-permute-start(f32[168,128]{1,0:T(8,128)S(1)} %shard_map.184.a), channel_id=1, source_target_pairs={{0,4},{2,6},{4,0},{6,2},{1,5},{3,7},{5,1},{7,3},{8,12},{10,14},{12... | collective-permute-start | bytes 258056 | tf_op jit(solution)/shard_map/ppermute | solution.py:236
  95.7 3.0 %collective-permute-done.15 = f32[8,128]{1,0:T(8,128)S(1)} collective-permute-done((f32[8,128]{1,0:T(8,128)S(1)}, f32[8,128]{1,0:T(8,128)S(1)}, u32[]{:S(2)}, u32[]{:S(2)}) %collective-permute-start.15) | collective-permute-done | bytes 4128 | tf_op jit(solution)/shard_map/ppermute | solution.py:240
  98.7 2.1 %collective-permute-start.16 = (f32[8,128]{1,0:T(8,128)S(1)}, f32[8,128]{1,0:T(8,128)S(1)}, u32[]{:S(2)}, u32[]{:S(2)}) collective-permute-start(f32[8,128]{1,0:T(8,128)S(1)} %add.19), channel_id=1, source_target_pairs={{0,16},{8,24},{16,0},{24,8},{1,17},{9,25},{17,1},{25,9},{2,18},{10... | collective-permute-start | bytes 12296 | tf_op jit(solution)/shard_map/ppermute | solution.py:240
  100.9 3.0 %collective-permute-done.16 = f32[8,128]{1,0:T(8,128)S(1)} collective-permute-done((f32[8,128]{1,0:T(8,128)S(1)}, f32[8,128]{1,0:T(8,128)S(1)}, u32[]{:S(2)}, u32[]{:S(2)}) %collective-permute-start.16) | collective-permute-done | bytes 4128 | tf_op jit(solution)/shard_map/ppermute | solution.py:240
  103.9 3.6 %collective-permute-done.17 = f32[8,128]{1,0:T(8,128)S(1)} collective-permute-done((f32[8,128]{1,0:T(8,128)S(1)}, f32[8,128]{1,0:T(8,128)S(1)}, u32[]{:S(2)}, u32[]{:S(2)}) %collective-permute-start.17) | collective-permute-done | bytes 4128 | tf_op jit(solution)/shard_map/ppermute | solution.py:240
  107.5 1.6 %collective-permute-start.18 = (f32[8,128]{1,0:T(8,128)S(1)}, f32[8,128]{1,0:T(8,128)S(1)}, u32[]{:S(2)}, u32[]{:S(2)}) collective-permute-start(f32[8,128]{1,0:T(8,128)S(1)} %add.21), channel_id=1, source_target_pairs={{0,64},{32,96},{64,0},{96,32},{128,192},{160,224},{192,128},{224,1... | collective-permute-start | bytes 12296 | tf_op jit(solution)/shard_map/ppermute | solution.py:240
  109.1 2.9 %collective-permute-done.18 = f32[8,128]{1,0:T(8,128)S(1)} collective-permute-done((f32[8,128]{1,0:T(8,128)S(1)}, f32[8,128]{1,0:T(8,128)S(1)}, u32[]{:S(2)}, u32[]{:S(2)}) %collective-permute-start.18) | collective-permute-done | bytes 4128 | tf_op jit(solution)/shard_map/ppermute | solution.py:240
  112.0 3.9 %collective-permute-start.19 = (f32[8,128]{1,0:T(8,128)S(1)}, f32[8,128]{1,0:T(8,128)S(1)}, u32[]{:S(2)}, u32[]{:S(2)}) collective-permute-start(f32[8,128]{1,0:T(8,128)S(1)} %add.22), channel_id=1, source_target_pairs={{0,128},{32,160},{64,192},{96,224},{128,0},{160,32},{192,64},{224,... | collective-permute-start | bytes 12296 | tf_op jit(solution)/shard_map/ppermute | solution.py:240
  115.9 3.6 %collective-permute-done.19 = f32[8,128]{1,0:T(8,128)S(1)} collective-permute-done((f32[8,128]{1,0:T(8,128)S(1)}, f32[8,128]{1,0:T(8,128)S(1)}, u32[]{:S(2)}, u32[]{:S(2)}) %collective-permute-start.19) | collective-permute-done | bytes 4128 | tf_op jit(solution)/shard_map/ppermute | solution.py:240
  120.9 5.8 %copy-done = bf16[8192,1024]{1,0:T(8,128)(2,1)S(1)} copy-done((bf16[8192,1024]{1,0:T(8,128)(2,1)S(1)}, bf16[8192,1024]{1,0:T(8,128)(2,1)}, u32[]{:S(2)}) %copy-start) | copy-done | bytes 16777240
  126.6 10.2 %shard_map.181 = bf16[256,8192]{1,0:T(8,128)(2,1)} custom-call(bf16[256,1024]{1,0:T(8,128)(2,1)S(1)} %copy-done.4, bf16[8192,1024]{1,0:T(8,128)(2,1)S(1)} %copy-done, bf16[256,128]{1,0:T(8,128)(2,1)S(1)} %get-tuple-element.30.back, bf16[8192,128]{1,0:T(8,128)(2,1)S(1)} %copy-done.2), custom_call_target="tpu_custom_call" | custom-call | flops 4831838208 | bytes 23068672 | tf_op jit(solution)/shard_map/pallas_call | solution.py:215
  (55 shorter events, 14.2 us)
Async XLA Ops:
  7.2 113.7 %all-gather.2.cloned.1.call-start = ((), (), s32[]{:S(2)}) async-start(), calls=%async_computation | async-start | bytes 17301504 | tf_op jit(solution)/shard_map/all_gather | solution.py:251
  8.0 1.6 %copy-start.1 = (bf16[8192,128]{1,0:T(8,128)(2,1)S(1)}, bf16[8192,128]{1,0:T(8,128)(2,1)}, u32[]{:S(2)}) copy-start(bf16[8192,128]{1,0:T(8,128)(2,1)} %down.1) | copy-start | bytes 6291460
  19.2 5.2 %collective-permute-start = (f32[32,160,128]{2,1,0:T(8,128)}, f32[32,160,128]{2,1,0:T(8,128)S(1)}, u32[]{:S(2)}, u32[]{:S(2)}) collective-permute-start(f32[32,160,128]{2,1,0:T(8,128)} %get-tuple-element.32), channel_id=1, source_target_pairs={{0,1},{1,0},{2,3},{3,2},{4,5},{5,4},{6,7},{7,6},{8,9},{9,8},{10,11... | collective-permute-start | bytes 7864328 | tf_op jit(solution)/shard_map/ppermute | solution.py:240
  25.9 58.0 %copy-start.12 = (s32[1,8]{1,0:T(1,128)S(1)}, s32[1,8]{1,0:T(1,128)}, u32[]{:S(2)}) copy-start(s32[1,8]{1,0:T(1,128)} %flags_ref.1) | copy-start | bytes 100
  25.9 93.6 %copy-start.6 = (f32[32,128]{1,0:T(8,128)S(1)}, f32[32,128]{1,0:T(8,128)}, u32[]{:S(2)}) copy-start(f32[32,128]{1,0:T(8,128)} %master_a.1) | copy-start | bytes 49156
  25.9 93.6 %copy-start.7 = (f32[32,128]{1,0:T(8,128)S(1)}, f32[32,128]{1,0:T(8,128)}, u32[]{:S(2)}) copy-start(f32[32,128]{1,0:T(8,128)} %moment_a.1) | copy-start | bytes 49156
  25.9 93.6 %copy-start.8 = (f32[32,128]{1,0:T(8,128)S(1)}, f32[32,128]{1,0:T(8,128)}, u32[]{:S(2)}) copy-start(f32[32,128]{1,0:T(8,128)} %second_a.1) | copy-start | bytes 49156
  25.9 93.6 %copy-start.9 = (f32[4,128]{1,0:T(4,128)S(1)}, f32[4,128]{1,0:T(4,128)}, u32[]{:S(2)}) copy-start(f32[4,128]{1,0:T(4,128)} %master_b.1) | copy-start | bytes 6148
  25.9 93.6 %copy-start.10 = (f32[4,128]{1,0:T(4,128)S(1)}, f32[4,128]{1,0:T(4,128)}, u32[]{:S(2)}) copy-start(f32[4,128]{1,0:T(4,128)} %moment_b.1) | copy-start | bytes 6148
  25.9 93.6 %copy-start.11 = (f32[4,128]{1,0:T(4,128)S(1)}, f32[4,128]{1,0:T(4,128)}, u32[]{:S(2)}) copy-start(f32[4,128]{1,0:T(4,128)} %second_b.1) | copy-start | bytes 6148
  25.9 94.9 %copy-start.2 = (bf16[8192,128]{1,0:T(8,128)(2,1)S(1)}, bf16[8192,128]{1,0:T(8,128)(2,1)}, u32[]{:S(2)}) copy-start(bf16[8192,128]{1,0:T(8,128)(2,1)} %down.1) | copy-start | bytes 6291460
  26.0 94.9 %copy-start.4 = (bf16[256,1024]{1,0:T(8,128)(2,1)S(1)}, bf16[256,1024]{1,0:T(8,128)(2,1)}, u32[]{:S(2)}) copy-start(bf16[256,1024]{1,0:T(8,128)(2,1)} %g.1) | copy-start | bytes 1572868
  28.5 12.8 %collective-permute-start.1 = (bf16[640,128]{1,0:T(8,128)(2,1)S(1)}, bf16[640,128]{1,0:T(8,128)(2,1)S(1)}, u32[]{:S(2)}, u32[]{:S(2)}) collective-permute-start(bf16[640,128]{1,0:T(8,128)(2,1)S(1)} %get-tuple-element.34), channel_id=1, source_target_pairs={{0,32},{32,64},{64,96},{96,128},{128,160},{160,192},{192,224},{224... | collective-permute-start | bytes 491528 | tf_op jit(solution)/shard_map/ppermute | solution.py:236
  30.4 15.8 %collective-permute-start.2 = (bf16[640,128]{1,0:T(8,128)(2,1)S(1)}, bf16[640,128]{1,0:T(8,128)(2,1)S(1)}, u32[]{:S(2)}, u32[]{:S(2)}) collective-permute-start(bf16[640,128]{1,0:T(8,128)(2,1)S(1)} %get-tuple-element.35), channel_id=1, source_target_pairs={{0,64},{32,96},{64,128},{96,160},{128,192},{160,224},{192,0},{224,... | collective-permute-start | bytes 491528 | tf_op jit(solution)/shard_map/ppermute | solution.py:236
  34.8 26.5 %collective-permute-start.3 = (bf16[640,128]{1,0:T(8,128)(2,1)S(1)}, bf16[640,128]{1,0:T(8,128)(2,1)S(1)}, u32[]{:S(2)}, u32[]{:S(2)}) collective-permute-start(bf16[640,128]{1,0:T(8,128)(2,1)S(1)} %get-tuple-element.36), channel_id=1, source_target_pairs={{0,96},{32,128},{64,160},{96,192},{128,224},{160,0},{192,32},{224,... | collective-permute-start | bytes 491528 | tf_op jit(solution)/shard_map/ppermute | solution.py:236
  36.7 24.6 %collective-permute-start.4 = (bf16[640,128]{1,0:T(8,128)(2,1)S(1)}, bf16[640,128]{1,0:T(8,128)(2,1)S(1)}, u32[]{:S(2)}, u32[]{:S(2)}) collective-permute-start(bf16[640,128]{1,0:T(8,128)(2,1)S(1)} %get-tuple-element.37), channel_id=1, source_target_pairs={{0,128},{32,160},{64,192},{96,224},{128,0},{160,32},{192,64},{224,... | collective-permute-start | bytes 491528 | tf_op jit(solution)/shard_map/ppermute | solution.py:236
  38.2 23.2 %collective-permute-start.5 = (bf16[640,128]{1,0:T(8,128)(2,1)S(1)}, bf16[640,128]{1,0:T(8,128)(2,1)S(1)}, u32[]{:S(2)}, u32[]{:S(2)}) collective-permute-start(bf16[640,128]{1,0:T(8,128)(2,1)S(1)} %get-tuple-element.38), channel_id=1, source_target_pairs={{0,160},{32,192},{64,224},{96,0},{128,32},{160,64},{192,96},{224,1... | collective-permute-start | bytes 491528 | tf_op jit(solution)/shard_map/ppermute | solution.py:236
  41.3 26.5 %collective-permute-start.6 = (bf16[640,128]{1,0:T(8,128)(2,1)S(1)}, bf16[640,128]{1,0:T(8,128)(2,1)S(1)}, u32[]{:S(2)}, u32[]{:S(2)}) collective-permute-start(bf16[640,128]{1,0:T(8,128)(2,1)S(1)} %get-tuple-element.39), channel_id=1, source_target_pairs={{0,192},{32,224},{64,0},{96,32},{128,64},{160,96},{192,128},{224,1... | collective-permute-start | bytes 491528 | tf_op jit(solution)/shard_map/ppermute | solution.py:236
  46.2 23.5 %collective-permute-start.7 = (bf16[640,128]{1,0:T(8,128)(2,1)S(1)}, bf16[640,128]{1,0:T(8,128)(2,1)S(1)}, u32[]{:S(2)}, u32[]{:S(2)}) collective-permute-start(bf16[640,128]{1,0:T(8,128)(2,1)S(1)} %get-tuple-element.40), channel_id=1, source_target_pairs={{0,224},{32,0},{64,32},{96,64},{128,96},{160,128},{192,160},{224,1... | collective-permute-start | bytes 491528 | tf_op jit(solution)/shard_map/ppermute | solution.py:236
  70.5 7.3 %collective-permute-start.10 = (f32[160,128]{1,0:T(8,128)S(1)}, f32[160,128]{1,0:T(8,128)S(1)}, u32[]{:S(2)}, u32[]{:S(2)}) collective-permute-start(f32[160,128]{1,0:T(8,128)S(1)} %get-tuple-element.44), channel_id=1, source_target_pairs={{0,24},{8,0},{16,8},{24,16},{1,25},{9,1},{17,9},{25,17},{2,26},{10... | collective-permute-start | bytes 245768 | tf_op jit(solution)/shard_map/ppermute | solution.py:236
  73.5 9.3 %collective-permute-start.8 = (f32[160,128]{1,0:T(8,128)S(1)}, f32[160,128]{1,0:T(8,128)S(1)}, u32[]{:S(2)}, u32[]{:S(2)}) collective-permute-start(f32[160,128]{1,0:T(8,128)S(1)} %get-tuple-element.42), channel_id=1, source_target_pairs={{0,8},{8,16},{16,24},{24,0},{1,9},{9,17},{17,25},{25,1},{2,10},{10... | collective-permute-start | bytes 245768 | tf_op jit(solution)/shard_map/ppermute | solution.py:236
  73.5 10.4 %collective-permute-start.9 = (f32[160,128]{1,0:T(8,128)S(1)}, f32[160,128]{1,0:T(8,128)S(1)}, u32[]{:S(2)}, u32[]{:S(2)}) collective-permute-start(f32[160,128]{1,0:T(8,128)S(1)} %get-tuple-element.43), channel_id=1, source_target_pairs={{0,16},{8,24},{16,0},{24,8},{1,17},{9,25},{17,1},{25,9},{2,18},{10... | collective-permute-start | bytes 245768 | tf_op jit(solution)/shard_map/ppermute | solution.py:236
  84.5 6.7 %collective-permute-start.11 = (f32[168,128]{1,0:T(8,128)S(1)}, f32[168,128]{1,0:T(8,128)S(1)}, u32[]{:S(2)}, u32[]{:S(2)}) collective-permute-start(f32[168,128]{1,0:T(8,128)S(1)} %shard_map.184.a), channel_id=1, source_target_pairs={{0,2},{2,4},{4,6},{6,0},{1,3},{3,5},{5,7},{7,1},{8,10},{10,12},{12... | collective-permute-start | bytes 258056 | tf_op jit(solution)/shard_map/ppermute | solution.py:236
  86.0 6.3 %collective-permute-start.12 = (f32[168,128]{1,0:T(8,128)S(1)}, f32[168,128]{1,0:T(8,128)S(1)}, u32[]{:S(2)}, u32[]{:S(2)}) collective-permute-start(f32[168,128]{1,0:T(8,128)S(1)} %shard_map.184.a), channel_id=1, source_target_pairs={{0,4},{2,6},{4,0},{6,2},{1,5},{3,7},{5,1},{7,3},{8,12},{10,14},{12... | collective-permute-start | bytes 258056 | tf_op jit(solution)/shard_map/ppermute | solution.py:236
  88.8 4.5 %collective-permute-start.13 = (f32[168,128]{1,0:T(8,128)S(1)}, f32[168,128]{1,0:T(8,128)S(1)}, u32[]{:S(2)}, u32[]{:S(2)}) collective-permute-start(f32[168,128]{1,0:T(8,128)S(1)} %shard_map.184.a), channel_id=1, source_target_pairs={{0,6},{2,0},{4,2},{6,4},{1,7},{3,1},{5,3},{7,5},{8,14},{10,8},{12,... | collective-permute-start | bytes 258056 | tf_op jit(solution)/shard_map/ppermute | solution.py:236
  93.9 1.3 collective-permute-start.14
  95.1 3.6 %collective-permute-start.15 = (f32[8,128]{1,0:T(8,128)S(1)}, f32[8,128]{1,0:T(8,128)S(1)}, u32[]{:S(2)}, u32[]{:S(2)}) collective-permute-start(f32[8,128]{1,0:T(8,128)S(1)} %add.18), channel_id=1, source_target_pairs={{0,8},{8,0},{16,24},{24,16},{1,9},{9,1},{17,25},{25,17},{2,10},{10... | collective-permute-start | bytes 12296 | tf_op jit(solution)/shard_map/ppermute | solution.py:240
  98.7 5.1 %collective-permute-start.16 = (f32[8,128]{1,0:T(8,128)S(1)}, f32[8,128]{1,0:T(8,128)S(1)}, u32[]{:S(2)}, u32[]{:S(2)}) collective-permute-start(f32[8,128]{1,0:T(8,128)S(1)} %add.19), channel_id=1, source_target_pairs={{0,16},{8,24},{16,0},{24,8},{1,17},{9,25},{17,1},{25,9},{2,18},{10... | collective-permute-start | bytes 12296 | tf_op jit(solution)/shard_map/ppermute | solution.py:240
  103.9 3.6 %collective-permute-start.17 = (f32[8,128]{1,0:T(8,128)S(1)}, f32[8,128]{1,0:T(8,128)S(1)}, u32[]{:S(2)}, u32[]{:S(2)}) collective-permute-start(f32[8,128]{1,0:T(8,128)S(1)} %add.20), channel_id=1, source_target_pairs={{0,32},{32,0},{64,96},{96,64},{128,160},{160,128},{192,224},{224,1... | collective-permute-start | bytes 12296 | tf_op jit(solution)/shard_map/ppermute | solution.py:240
  107.5 4.5 %collective-permute-start.18 = (f32[8,128]{1,0:T(8,128)S(1)}, f32[8,128]{1,0:T(8,128)S(1)}, u32[]{:S(2)}, u32[]{:S(2)}) collective-permute-start(f32[8,128]{1,0:T(8,128)S(1)} %add.21), channel_id=1, source_target_pairs={{0,64},{32,96},{64,0},{96,32},{128,192},{160,224},{192,128},{224,1... | collective-permute-start | bytes 12296 | tf_op jit(solution)/shard_map/ppermute | solution.py:240
  112.0 7.5 %collective-permute-start.19 = (f32[8,128]{1,0:T(8,128)S(1)}, f32[8,128]{1,0:T(8,128)S(1)}, u32[]{:S(2)}, u32[]{:S(2)}) collective-permute-start(f32[8,128]{1,0:T(8,128)S(1)} %add.22), channel_id=1, source_target_pairs={{0,128},{32,160},{64,192},{96,224},{128,0},{160,32},{192,64},{224,... | collective-permute-start | bytes 12296 | tf_op jit(solution)/shard_map/ppermute | solution.py:240
  120.8 5.8 %copy-start = (bf16[8192,1024]{1,0:T(8,128)(2,1)S(1)}, bf16[8192,1024]{1,0:T(8,128)(2,1)}, u32[]{:S(2)}) copy-start(bf16[8192,1024]{1,0:T(8,128)(2,1)} %all-gather.2.cloned.1.call-done.weight) | copy-start | bytes 50331652
  (4 other events, 4.1 us)
Sparse Core Ops, SparseCore 0:
  10.6 83.6 all-gather.1

commit v2 on v1

v2 whole, which is shorter than its diff:
```python
import functools

import jax
import jax.numpy as jnp
from jax import lax
from jax.experimental import pallas as pl
from jax.experimental.pallas import tpu as pltpu
from jax.sharding import Mesh
from jax.sharding import PartitionSpec as P

ADAPTER_SCALE = 2.0
BETA_ONE = 0.9
BETA_TWO = 0.95
LEARN_RATE = 0.002
ADAM_EPS = 1e-08

DEV = ("z", "y", "x", "c")
PLANE = ("y", "x", "c")
F32 = jnp.float32
BF16 = jnp.bfloat16
CONTRACT_LAST = (((1,), (1,)), ((), ()))
CONTRACT_FIRST = (((0,), (0,)), ((), ()))

VMEM = pl.BlockSpec(memory_space=pltpu.VMEM)
SMEM = pl.BlockSpec(memory_space=pltpu.SMEM)
HBM = pl.BlockSpec(memory_space=pl.ANY)


def call(kernel, outs, ins, scratch=(), limit=48, flops=0, nbytes=0, to=None):
    return pl.pallas_call(
        kernel,
        out_shape=outs,
        in_specs=ins,
        out_specs=jax.tree.map(lambda _: VMEM, outs) if to is None else to,
        scratch_shapes=list(scratch),
        compiler_params=pltpu.CompilerParams(vmem_limit_bytes=limit << 20),
        cost_estimate=pl.CostEstimate(flops=flops, bytes_accessed=nbytes, transcendentals=0),
    )


def grads_kernel(
    where_ref, counts_ref, tok_hbm, g_hbm, down_hbm, up_hbm,
    keep_hbm, send_hbm, back_ref,
    tok, g, down, up, keep_ref, send_ref, sems, small_sems, out_sems,
):
    rows, width = tok.shape
    kv = g.shape[1]
    cols = down.shape[1]
    adapters = counts_ref.shape[1]
    rank = cols // adapters
    tiles = sems.shape[0]
    tile = width // tiles
    blocks, nx = keep_ref.shape[:2]
    block = width // blocks
    half = block // nx // 2
    few = kv // blocks // nx
    first = where_ref[3] == 0

    g_copy = pltpu.make_async_copy(g_hbm, g, small_sems.at[0])
    up_copy = pltpu.make_async_copy(up_hbm, up, small_sems.at[1])
    g_copy.start()
    up_copy.start()
    tok_copies = []
    for t in range(tiles):
        span = pl.ds(t * tile, tile)
        a = pltpu.make_async_copy(tok_hbm.at[:, span], tok.at[:, span], sems.at[t, 0])
        b = pltpu.make_async_copy(down_hbm.at[span, :], down.at[span, :], sems.at[t, 1])
        a.start()
        b.start()
        tok_copies.append((a, b))

    row_ids = lax.broadcasted_iota(jnp.int32, (rows, cols), 0)
    col_owner = lax.broadcasted_iota(jnp.int32, (rows, cols), 1) // rank
    owner = jnp.zeros((rows, cols), jnp.int32)
    end = jnp.int32(0)
    for e in range(adapters):
        end = end + counts_ref[0, e]
        owner = owner + (row_ids >= end).astype(jnp.int32)
    mask = (owner == col_owner).astype(F32)

    g_copy.wait()
    up_copy.wait()
    back = (
        ADAPTER_SCALE * jnp.dot(g[...], up[...], preferred_element_type=F32) * mask
    ).astype(BF16)
    back_ref[...] = back

    acc = jnp.zeros((rows, cols), F32)
    for t in range(tiles):
        tok_copies[t][0].wait()
        tok_copies[t][1].wait()
        span = slice(t * tile, (t + 1) * tile)
        acc = acc + jnp.dot(tok[:, span], down[span, :], preferred_element_type=F32)
    low = (ADAPTER_SCALE * acc * mask).astype(BF16)
    group = block // (few * nx)
    for s in range(kv // block):
        r = lax.dot_general(
            g[:, s * block : (s + 1) * block], low, CONTRACT_FIRST, preferred_element_type=F32
        ).reshape(group, nx, few, cols)
        keep_ref[s * group : (s + 1) * group, :, half:] = r
        send_ref[s * group : (s + 1) * group, :, half:] = r.astype(BF16)
    per = blocks // tiles
    stores = []
    for t in range(tiles):
        for b in range(t * per, (t + 1) * per):
            r = lax.dot_general(
                tok[:, b * block : (b + 1) * block], back, CONTRACT_FIRST,
                preferred_element_type=F32,
            ).reshape(nx, 2, half, cols)
            keep_ref[b, :, :half] = jnp.where(first, r[:, 0], r[:, 1])
            send_ref[b, :, :half] = jnp.where(first, r[:, 1], r[:, 0]).astype(BF16)
        span = pl.ds(t * per, per)
        for i, (src, dst) in enumerate(((send_ref, send_hbm), (keep_ref, keep_hbm))):
            stores.append(pltpu.make_async_copy(src.at[span], dst.at[span], out_sems.at[t, i]))
            stores[-1].start()
    for copy in stores:
        copy.wait()


def plane_sum_kernel(parts, out):
    total = parts[0].astype(F32)
    for z in range(1, parts.shape[0]):
        total = total + parts[z].astype(F32)
    out[...] = total


def squares_kernel(where_ref, flags_ref, parts, total_ref, share_ref):
    deep, cols = total_ref.shape
    wide = deep * 4 // 5
    adapters = flags_ref.shape[1]
    rank = cols // adapters
    total = jnp.sum(parts[...], axis=0)
    total_ref[...] = total
    part_a = total[:wide]
    part_b = total[wide:]
    owner = lax.broadcasted_iota(jnp.int32, part_b.shape, 0) // 4
    part_b = jnp.where(owner == where_ref[3], part_b, 0.0)
    squares = jnp.sum(part_a * part_a, axis=0, keepdims=True) + jnp.sum(
        part_b * part_b, axis=0, keepdims=True
    )
    lane = lax.broadcasted_iota(jnp.int32, (1, cols), 1)
    row = jnp.zeros((1, cols), F32)
    for e in range(adapters):
        mine = lane // rank == e
        one = jnp.sum(jnp.where(mine, squares, 0.0), axis=1, keepdims=True)
        row = jnp.where(mine, jnp.where(lane % rank == 0, one, flags_ref[0, e].astype(F32)), row)
    share_ref[...] = jnp.broadcast_to(row[None], share_ref.shape)


def adam_kernel(
    limit_sq, where_ref, total_ref, shares_ref,
    master_a, moment_a, second_a, master_b, moment_b, second_b,
    out_ma, out_oa, out_sa, out_mb, out_ob, out_sb,
):
    rows, cols = master_a.shape
    adapters = 8
    rank = cols // adapters
    row = jnp.sum(shares_ref[...], axis=0)
    lane = lax.broadcasted_iota(jnp.int32, (1, cols), 1)
    sums = jnp.zeros((1, cols), F32)
    flags = jnp.zeros((1, cols), F32)
    for e in range(adapters):
        mine = lane // rank == e
        one = jnp.sum(jnp.where(lane == e * rank, row, 0.0), axis=1, keepdims=True)
        flag = jnp.sum(jnp.where(lane == e * rank + 1, row, 0.0), axis=1, keepdims=True)
        sums = jnp.where(mine, one, sums)
        flags = jnp.where(mine, flag, flags)
    limit = jnp.sqrt(jnp.full((1, cols), limit_sq, F32))
    clip = limit / jnp.maximum(jnp.sqrt(sums), limit)
    held = flags > 0.5

    def commit(grad, master, moment, second, to_master, to_moment, to_second):
        clipped = grad * clip
        m, o, s = master[...], moment[...], second[...]
        new_o = BETA_ONE * o + (1.0 - BETA_ONE) * clipped
        new_s = BETA_TWO * s + (1.0 - BETA_TWO) * clipped * clipped
        new_m = m - LEARN_RATE * new_o / (jnp.sqrt(new_s) + ADAM_EPS)
        to_master[...] = jnp.where(held, m, new_m)
        to_moment[...] = jnp.where(held, o, new_o)
        to_second[...] = jnp.where(held, s, new_s)

    grad_a = total_ref[:rows]
    pair = total_ref[rows:]
    grad_b = jnp.where(where_ref[3] == 0, pair[:4], pair[4:])
    commit(grad_a, master_a, moment_a, second_a, out_ma, out_oa, out_sa)
    commit(grad_b, master_b, moment_b, second_b, out_mb, out_ob, out_sb)


def input_grad_kernel(
    g_hbm, weight_hbm, back_hbm, down_hbm, out_hbm, g, weight, out, sems, out_sems
):
    chunks, tile = weight.shape[:2]
    kv = g_hbm.shape[1]
    main, side = pl.ds(0, kv), pl.ds(kv, back_hbm.shape[1])
    small = [
        pltpu.make_async_copy(g_hbm, g.at[:, main], sems.at[2 * chunks]),
        pltpu.make_async_copy(back_hbm, g.at[:, side], sems.at[2 * chunks + 1]),
    ]

    def loads(i):
        rows = pl.ds(pl.multiple_of(i * tile, tile), tile)
        return (
            pltpu.make_async_copy(weight_hbm.at[rows], weight.at[i, :, main], sems.at[i]),
            pltpu.make_async_copy(down_hbm.at[rows], weight.at[i, :, side], sems.at[chunks + i]),
        )

    def store(i):
        cols = pl.ds(pl.multiple_of(i * tile, tile), tile)
        return pltpu.make_async_copy(out.at[i], out_hbm.at[:, cols], out_sems.at[i])

    for copy in small:
        copy.start()
    for i in range(chunks):
        for copy in loads(i):
            copy.start()
    for copy in small:
        copy.wait()

    def step(i, carry):
        for copy in loads(i):
            copy.wait()
        total = lax.dot_general(g[...], weight[i], CONTRACT_LAST, preferred_element_type=F32)
        out[i] = total.astype(BF16)
        store(i).start()
        return carry

    lax.fori_loop(0, chunks, step, 0)
    for i in range(chunks):
        store(i).wait()


def input_grad(g, weight, back, down, tile):
    rows, kv = g.shape
    width, cols = down.shape
    chunks = width // tile
    return pl.pallas_call(
        input_grad_kernel,
        out_shape=jax.ShapeDtypeStruct((rows, width), BF16),
        in_specs=[HBM] * 4,
        out_specs=HBM,
        scratch_shapes=[
            pltpu.VMEM((rows, kv + cols), BF16),
            pltpu.VMEM((chunks, tile, kv + cols), BF16),
            pltpu.VMEM((chunks, rows, tile), BF16),
            pltpu.SemaphoreType.DMA((2 * chunks + 2,)),
            pltpu.SemaphoreType.DMA((chunks,)),
        ],
        compiler_params=pltpu.CompilerParams(vmem_limit_bytes=60 << 20),
        cost_estimate=pl.CostEstimate(
            flops=2 * rows * width * (kv + cols),
            bytes_accessed=2 * width * (kv + cols + rows),
            transcendentals=0,
        ),
    )(g, weight, back, down)


def shift(value, axis, size, by):
    return lax.ppermute(value, axis, [(i, (i + by) % size) for i in range(size)])


def flip(value, axis, size, bit):
    return lax.ppermute(value, axis, [(i, i ^ bit) for i in range(size)])


def shards(sizes, tokens, g, base_weight, down, up, ma, oa, sa, mb, ob, sb, counts, flags):
    nz, ny, nx, nc = sizes
    rows, width = tokens.shape
    kv = g.shape[1]
    cols = down.shape[1]
    where = jnp.stack([lax.axis_index(a) for a in DEV]).astype(jnp.int32)
    sds = jax.ShapeDtypeStruct

    weight = lax.all_gather(base_weight, PLANE, axis=0, tiled=True)

    blocks = nz * ny
    deep = width // blocks // nx // nc + kv // blocks // nx
    part = (blocks, nx, deep, cols)
    tiles = 8
    keep, send, back = call(
        grads_kernel,
        (sds(part, F32), sds(part, BF16), sds((rows, cols), BF16)),
        [SMEM, SMEM, HBM, HBM, HBM, HBM],
        [
            pltpu.VMEM((rows, width), BF16),
            pltpu.VMEM((rows, kv), BF16),
            pltpu.VMEM((width, cols), BF16),
            pltpu.VMEM((kv, cols), BF16),
            pltpu.VMEM(part, F32),
            pltpu.VMEM(part, BF16),
            pltpu.SemaphoreType.DMA((tiles, 2)),
            pltpu.SemaphoreType.DMA((2,)),
            pltpu.SemaphoreType.DMA((tiles, 2)),
        ],
        limit=60,
        to=(HBM, HBM, VMEM),
        flops=4 * rows * width * cols,
        nbytes=12 << 20,
    )(where, counts, tokens, g, down, up)

    recv = flip(send, "c", nc, 1)
    to_all = (keep + recv.astype(F32)).astype(BF16)
    chips = nz * ny * nx
    from_z = lax.all_to_all(to_all.reshape(nz, ny * nx, deep, cols), "z", 0, 0, tiled=True)
    to_plane = call(plane_sum_kernel, sds((ny * nx, deep, cols), F32), [VMEM], nbytes=2 << 20)(from_z)
    from_all = lax.all_to_all(to_plane, ("y", "x"), 0, 0, tiled=True)

    total, share = call(
        squares_kernel,
        (sds((deep, cols), F32), sds((chips * nc, 1, cols), F32)),
        [SMEM, SMEM, VMEM],
    )(where, flags, from_all)
    weight, _ = lax.optimization_barrier((weight, share))
    shares = lax.all_to_all(share, DEV, 0, 0, tiled=True)
    out = input_grad(g, weight, back, down, 512)
    shares, out = lax.optimization_barrier((shares, out))

    shape = lambda v: sds(v.shape, v.dtype)
    new = call(
        functools.partial(adam_kernel, float(cols // 8 * (width + kv))),
        tuple(shape(v) for v in (ma, oa, sa, mb, ob, sb)),
        [SMEM] + [VMEM] * 8,
    )(where, total, shares, ma, oa, sa, mb, ob, sb)
    return (out, *new)


def solution(mesh):
    sizes = (8, 4, 4, 2)
    fine = Mesh(mesh.devices.reshape(sizes), DEV)
    split = P(DEV, None)
    return jax.shard_map(
        functools.partial(shards, sizes),
        mesh=fine,
        in_specs=(split, split, P(PLANE, None), P(), P()) + (split,) * 8,
        out_specs=(split,) * 7,
        check_vma=False,
    )
```

time: 144 us -> 117 us (0.81); the launches traced: 144 us -> 115 us
  blocking collectives: 0 us -> 61.6 us
  waiting for transfers between devices: 57.4 us -> 5.04 us
  starting transfers between devices: 37.6 us -> 7.25 us
  local copies, waits for them, and re-layouts: 11.5 us -> 0.04 us
  other arithmetic: 0.1 us -> 2.72 us
    all_to_all x0 -> x2, blocking collectives: none -> 61.6 us  [the longest x1 41.7 us: shards(): lax.all_to_all(to_all.reshape(nz, ny * nx, deep, cols), 'z', 0, 0, tiled=...]
    ppermute x13 -> x0, waiting for transfers between devices: 34.4 us -> none  [shift(): lax.ppermute(value, axis, [(i, (i + by) % size) for i in range(size)])]
    ppermute x13 -> x0, starting transfers between devices: 29.1 us -> none  [shift(): lax.ppermute(value, axis, [(i, (i + by) % size) for i in range(size)])]
    ppermute x7 -> x1, waiting for transfers between devices: 22.3 us -> 3.23 us  [flip(): return lax.ppermute(value, axis, [(i, i ^ bit) for i in range(size)])]
    unnamed x30 -> x16, local copies, waits for them, and re-layouts: 11.5 us -> 0.04 us
    ppermute x7 -> x1, starting transfers between devices: 8.47 us -> 0.09 us  [flip(): return lax.ppermute(value, axis, [(i, i ^ bit) for i in range(size)])]
    all_to_all x0 -> x1, starting transfers between devices: none -> 7.13 us  [shards(): shares = lax.all_to_all(share, DEV, 0, 0, tiled=True)]
    convert_element_type x0 -> x1, other arithmetic: none -> 2.13 us  [shards(): to_all = (keep + recv.astype(F32)).astype(BF16)]
  transfers between devices with their start and end apart: 21 -> 3, of which waited for: 17 -> 3; matrix products, arithmetic and copies ran while one was open for 0% -> 2% of each run, Pallas kernels for 9% -> 19%
where the time goes in v2:
time: 117 us; the launch traced here: 115 us
  blocking collectives  61.6 us (53%)
  Pallas kernels  23.7 us (20%)
  between operations  14.1 us (12%)
  starting transfers between devices  7.25 us (6%)
  waiting for transfers between devices  5.04 us (4%)
  other arithmetic  2.72 us (2%)
    all_to_all x1, blocking collectives, shards(): lax.all_to_all(to_all.reshape(nz, ny * nx, deep, cols), 'z', 0, 0, tiled=...  41.7 us
    all_to_all x1, blocking collectives, shards(): from_all = lax.all_to_all(to_plane, ('y', 'x'), 0, 0, tiled=True)  19.9 us
    pallas_call x1, Pallas kernels, input_grad(): pl.pallas_call(input_grad_kernel, out_shape=jax.ShapeDtypeStruct((rows, w...  11.3 us
    pallas_call x1, Pallas kernels, shards(): call(grads_kernel, (sds(part, F32), sds(part, BF16), sds((rows, cols), BF...  9.37 us
    all_to_all x1, starting transfers between devices, shards(): shares = lax.all_to_all(share, DEV, 0, 0, tiled=True)  7.13 us
    ppermute x1, waiting for transfers between devices, flip(): return lax.ppermute(value, axis, [(i, i ^ bit) for i in range(size)])  3.23 us
  transfers between devices with their start and end apart: 3, of which 3 were waited for; matrix products, arithmetic and copies ran while one was open for 2% of the time, Pallas kernels for 19%

profile of v2, /device:TPU:32, one launch (start us, length us, event | category | flops | bytes accessed | tf_op | source)
XLA Modules:
  0.0 114.5 jit_solution(4442411375074420814)
XLA Ops:
  7.2 0.0 all-gather.2.cloned.1.call-start
  7.2 0.7 all-gather.2.cloned.1.call-update
  7.9 0.6 pad_add_fusion.where_ref
  8.5 9.4 %shard_map.180 = (f32[32,4,40,128]{3,2,1,0:T(8,128)}, bf16[32,4,40,128]{3,2,1,0:T(8,128)(2,1)}, bf16[256,128]{1,0:T(8,128)(2,1)}) custom-call(s32[4]{0:T(128)} %pad_add_fusion.where_ref, s32[1,8]{1,0:T(1,128)} %counts_ref.1, bf16[256,8192]{1,0:T(8,128)(2,1)} %tok_hbm.1, bf16[256,1024]{1,0:T(8,128)(2,1)} %g_hbm.3, bf16[8192,128]{1,0:T(8,128)(2,1)} %down_hbm.3, ...), custom_call_target="tpu_custom_call" | custom-call | flops 1073741824 | bytes 12582912 | tf_op jit(solution)/shard_map/pallas_call | solution.py:279
  17.9 0.1 collective-permute-start
  18.0 3.2 %collective-permute-done = bf16[32,4,40,128]{3,2,1,0:T(8,128)(2,1)S(1)} collective-permute-done((bf16[32,4,40,128]{3,2,1,0:T(8,128)(2,1)}, bf16[32,4,40,128]{3,2,1,0:T(8,128)(2,1)S(1)}, u32[]{:S(2)}, u32[]{:S(2)}) %collective-permute-start) | collective-permute-done | bytes 1310752 | tf_op jit(solution)/shard_map/ppermute | solution.py:262
  21.2 2.1 %add_convert_fusion = bf16[32,4,40,128]{3,2,1,0:T(8,128)(2,1)S(1)} fusion(f32[32,4,40,128]{3,2,1,0:T(8,128)} %get-tuple-element.21, bf16[32,4,40,128]{3,2,1,0:T(8,128)(2,1)S(1)} %collective-permute-done), kind=kLoop, calls=%fused_computation | loop fusion | flops 1966080 | bytes 5242880 | tf_op jit(solution)/shard_map/convert_element_type | solution.py:301
  23.3 0.0 copy-start.3
  23.4 0.0 copy-start.7
  23.4 41.7 %all_to_all.15.parts = bf16[8,16,40,128]{3,2,1,0:T(8,128)(2,1)S(1)} all-to-all(bf16[8,16,40,128]{3,2,1,0:T(8,128)(2,1)S(1)} %bitcast.5), channel_id=1, replica_groups=mesh['z'=8,'y'=4,'x'=4,'c'=2] {'z'}, dimensions={0} | all-to-all | bytes 2621440 | tf_op jit(solution)/shard_map/all_to_all | solution.py:303
  65.1 0.2 shard_map.181
  65.2 19.9 %all_to_all.16.parts = f32[16,40,128]{2,1,0:T(8,128)S(1)} all-to-all(f32[16,40,128]{2,1,0:T(8,128)S(1)} %shard_map.181), channel_id=1, replica_groups=mesh['z'=8,'y'=4,'x'=4,'c'=2] {'y','x'}, dimensions={0} | all-to-all | bytes 655360 | tf_op jit(solution)/shard_map/all_to_all | solution.py:305
  85.1 0.0 copy-done.3
  85.1 0.0 copy-done.7
  85.1 1.4 %shard_map.182 = (f32[40,128]{1,0:T(8,128)S(1)}, f32[256,1,128]{2,1,0:T(1,128)}) custom-call(s32[4]{0:T(128)S(1)} %copy-done.3, s32[1,8]{1,0:T(1,128)S(1)} %copy-done.7, f32[16,40,128]{2,1,0:T(8,128)S(1)} %all_to_all.16.parts), custom_call_target="tpu_custom_call" | custom-call | tf_op jit(solution)/shard_map/pallas_call | solution.py:307
  86.5 7.1 %all-to-all-start.2 = ((f32[256,1,128]{2,1,0:T(1,128)}), f32[256,1,128]{2,1,0:T(1,128)S(1)}, u32[]{:S(2)}, u32[]{:S(2)}) async-start(f32[256,1,128]{2,1,0:T(1,128)} %get-tuple-element.23), calls=%async_computation.2 | async-start | bytes 262144 | tf_op jit(solution)/shard_map/all_to_all | solution.py:313
  93.6 0.6 all-gather.2.cloned.1.call-done.weight_hbm
  94.2 0.0 copy-start
  94.2 0.0 copy-start.1
  94.2 0.0 copy-start.2
  94.2 0.0 copy-start.4
  94.2 0.0 copy-start.5
  94.2 0.0 copy-start.6
  94.2 11.3 %shard_map.183 = bf16[256,8192]{1,0:T(8,128)(2,1)} custom-call(bf16[256,1024]{1,0:T(8,128)(2,1)} %g_hbm.3, bf16[8192,1024]{1,0:T(8,128)(2,1)} %all-gather.2.cloned.1.call-done.weight_hbm, bf16[256,128]{1,0:T(8,128)(2,1)} %get-tuple-element.25.back_hbm, bf16[8192,128]{1,0:T(8,128)(2,1)} %down_hbm.3), custom_call_target="tpu_custom_call" | custom-call | flops 4831838208 | bytes 23068672 | tf_op jit(solution)/shard_map/pallas_call | solution.py:236
  105.5 0.6 all-to-all-done.2.shares_ref
  106.1 0.0 copy-done
  106.1 0.0 copy-done.1
  106.1 0.0 copy-done.2
  106.1 0.0 copy-done.4
  106.1 0.0 copy-done.5
  106.1 0.0 copy-done.6
  106.1 1.6 %shard_map.184 = (f32[32,128]{1,0:T(8,128)}, f32[32,128]{1,0:T(8,128)}, f32[32,128]{1,0:T(8,128)}, f32[4,128]{1,0:T(4,128)}, f32[4,128]{1,0:T(4,128)}, /*index=5*/f32[4,128]{1,0:T(4,128)}) custom-call(s32[4]{0:T(128)S(1)} %copy-done.3, f32[40,128]{1,0:T(8,128)S(1)} %get-tuple-element.27.total_ref, f32[256,1,128]{2,1,0:T(1,128)S(1)} %all-to-all-done.2.shares_ref, ...), custom_call_target="tpu_custom_call" | custom-call | tf_op jit(solution)/shard_map/pallas_call | solution.py:318
Async XLA Ops:
  7.2 87.0 %all-gather.2.cloned.1.call-start = ((), (), s32[]{:S(2)}) async-start(), calls=%async_computation.3 | async-start | bytes 17301504 | tf_op jit(solution)/shard_map/all_gather | solution.py:273
  17.9 3.3 %collective-permute-start = (bf16[32,4,40,128]{3,2,1,0:T(8,128)(2,1)}, bf16[32,4,40,128]{3,2,1,0:T(8,128)(2,1)S(1)}, u32[]{:S(2)}, u32[]{:S(2)}) collective-permute-start(bf16[32,4,40,128]{3,2,1,0:T(8,128)(2,1)} %get-tuple-element.22), channel_id=1, source_target_pairs={{0,1},{1,0},{2,3},{3,2},{4,5},{5,4},{6,7},{7,6},{8,9},{9,8},{10,11... | collective-permute-start | bytes 3932168 | tf_op jit(solution)/shard_map/ppermute | solution.py:262
  23.3 61.8 %copy-start.3 = (s32[4]{0:T(128)S(1)}, s32[4]{0:T(128)}, u32[]{:S(2)}) copy-start(s32[4]{0:T(128)} %pad_add_fusion.where_ref) | copy-start | bytes 52
  23.4 61.8 %copy-start.7 = (s32[1,8]{1,0:T(1,128)S(1)}, s32[1,8]{1,0:T(1,128)}, u32[]{:S(2)}) copy-start(s32[1,8]{1,0:T(1,128)} %flags_ref.1) | copy-start | bytes 100
  86.5 19.6 %all-to-all-start.2 = ((f32[256,1,128]{2,1,0:T(1,128)}), f32[256,1,128]{2,1,0:T(1,128)S(1)}, u32[]{:S(2)}, u32[]{:S(2)}) async-start(f32[256,1,128]{2,1,0:T(1,128)} %get-tuple-element.23), calls=%async_computation.2 | async-start | bytes 262144 | tf_op jit(solution)/shard_map/all_to_all | solution.py:313
  94.2 11.9 %copy-start = (f32[32,128]{1,0:T(8,128)S(1)}, f32[32,128]{1,0:T(8,128)}, u32[]{:S(2)}) copy-start(f32[32,128]{1,0:T(8,128)} %master_a.1) | copy-start | bytes 49156
  94.2 11.9 %copy-start.1 = (f32[32,128]{1,0:T(8,128)S(1)}, f32[32,128]{1,0:T(8,128)}, u32[]{:S(2)}) copy-start(f32[32,128]{1,0:T(8,128)} %moment_a.1) | copy-start | bytes 49156
  94.2 11.9 %copy-start.2 = (f32[32,128]{1,0:T(8,128)S(1)}, f32[32,128]{1,0:T(8,128)}, u32[]{:S(2)}) copy-start(f32[32,128]{1,0:T(8,128)} %second_a.1) | copy-start | bytes 49156
  94.2 11.9 %copy-start.4 = (f32[4,128]{1,0:T(4,128)S(1)}, f32[4,128]{1,0:T(4,128)}, u32[]{:S(2)}) copy-start(f32[4,128]{1,0:T(4,128)} %master_b.1) | copy-start | bytes 6148
  94.2 11.9 %copy-start.5 = (f32[4,128]{1,0:T(4,128)S(1)}, f32[4,128]{1,0:T(4,128)}, u32[]{:S(2)}) copy-start(f32[4,128]{1,0:T(4,128)} %moment_b.1) | copy-start | bytes 6148
  94.2 11.9 %copy-start.6 = (f32[4,128]{1,0:T(4,128)S(1)}, f32[4,128]{1,0:T(4,128)}, u32[]{:S(2)}) copy-start(f32[4,128]{1,0:T(4,128)} %second_b.1) | copy-start | bytes 6148
Sparse Core Ops, SparseCore 0:
  10.6 83.6 all-gather.1

commit v3 on v2

--- a/solution.py
+++ b/solution.py
@@ -14,7 +14,7 @@
 LEARN_RATE = 0.002
 ADAM_EPS = 1e-08
 
-DEV = ("z", "y", "x", "c")
+DEV = ("far", "near", "y", "x", "c")
 PLANE = ("y", "x", "c")
 F32 = jnp.float32
 BF16 = jnp.bfloat16
@@ -54,7 +54,7 @@
     block = width // blocks
     half = block // nx // 2
     few = kv // blocks // nx
-    first = where_ref[3] == 0
+    first = where_ref[4] == 0
 
     g_copy = pltpu.make_async_copy(g_hbm, g, small_sems.at[0])
     up_copy = pltpu.make_async_copy(up_hbm, up, small_sems.at[1])
@@ -117,6 +117,51 @@
         copy.wait()
 
 
+def split_kernel(where_ref, keep_ref, recv_ref, own_ref, up_ref, down_ref):
+    near = where_ref[1]
+    own_ref[0] = keep_ref[0, near] + recv_ref[0, near].astype(F32)
+    other = (keep_ref[0, 1 - near] + recv_ref[0, 1 - near].astype(F32)).astype(BF16)
+    low = pl.program_id(0) < pl.num_programs(0) // 2
+
+    @pl.when(low)
+    def _():
+        up_ref[0] = other
+
+    @pl.when(jnp.logical_not(low))
+    def _():
+        down_ref[0] = other
+
+
+def split(where, keep, recv):
+    count, pair = keep.shape[:2]
+    rest = keep.shape[2:]
+    half = count // 2
+    zeros = (0,) * len(rest)
+    sds = jax.ShapeDtypeStruct
+    whole = pl.BlockSpec((1, pair) + rest, lambda i: (i, 0) + zeros)
+    return pl.pallas_call(
+        split_kernel,
+        grid=(count,),
+        out_shape=(
+            sds((count,) + rest, F32), sds((half,) + rest, BF16), sds((half,) + rest, BF16),
+        ),
+        in_specs=[SMEM, whole, whole],
+        out_specs=(
+            pl.BlockSpec((1,) + rest, lambda i: (i,) + zeros),
+            pl.BlockSpec((1,) + rest, lambda i: (jnp.minimum(i, half - 1),) + zeros),
+            pl.BlockSpec((1,) + rest, lambda i: (jnp.maximum(i - half, 0),) + zeros),
+        ),
+        compiler_params=pltpu.CompilerParams(vmem_limit_bytes=48 << 20),
+        cost_estimate=pl.CostEstimate(flops=0, bytes_accessed=6 << 20, transcendentals=0),
+    )(where, keep, recv)
+
+
+def merge_kernel(own_ref, low_ref, high_ref, out_ref):
+    half = low_ref.shape[0]
+    out_ref[:half] = (own_ref[:half] + low_ref[...].astype(F32)).astype(BF16)
+    out_ref[half:] = (own_ref[half:] + high_ref[...].astype(F32)).astype(BF16)
+
+
 def plane_sum_kernel(parts, out):
     total = parts[0].astype(F32)
     for z in range(1, parts.shape[0]):
@@ -134,7 +179,7 @@
     part_a = total[:wide]
     part_b = total[wide:]
     owner = lax.broadcasted_iota(jnp.int32, part_b.shape, 0) // 4
-    part_b = jnp.where(owner == where_ref[3], part_b, 0.0)
+    part_b = jnp.where(owner == where_ref[4], part_b, 0.0)
     squares = jnp.sum(part_a * part_a, axis=0, keepdims=True) + jnp.sum(
         part_b * part_b, axis=0, keepdims=True
     )
@@ -181,7 +226,7 @@
 
     grad_a = total_ref[:rows]
     pair = total_ref[rows:]
-    grad_b = jnp.where(where_ref[3] == 0, pair[:4], pair[4:])
+    grad_b = jnp.where(where_ref[4] == 0, pair[:4], pair[4:])
     commit(grad_a, master_a, moment_a, second_a, out_ma, out_oa, out_sa)
     commit(grad_b, master_b, moment_b, second_b, out_mb, out_ob, out_sb)
 
@@ -263,7 +308,8 @@
 
 
 def shards(sizes, tokens, g, base_weight, down, up, ma, oa, sa, mb, ob, sb, counts, flags):
-    nz, ny, nx, nc = sizes
+    nf, nn, ny, nx, nc = sizes
+    nz = nf * nn
     rows, width = tokens.shape
     kv = g.shape[1]
     cols = down.shape[1]
@@ -298,12 +344,17 @@
     )(where, counts, tokens, g, down, up)
 
     recv = flip(send, "c", nc, 1)
-    to_all = (keep + recv.astype(F32)).astype(BF16)
     chips = nz * ny * nx
-    from_z = lax.all_to_all(to_all.reshape(nz, ny * nx, deep, cols), "z", 0, 0, tiled=True)
-    to_plane = call(plane_sum_kernel, sds((ny * nx, deep, cols), F32), [VMEM], nbytes=2 << 20)(from_z)
+    fine = (nf, nn, ny * nx, deep, cols)
+    own, up, low = split(where, keep.reshape(fine), recv.reshape(fine))
+    z_axes = ("far", "near")
+    from_below, from_above = shift(up, z_axes, nz, 1), shift(low, z_axes, nz, -1)
+    merged = call(merge_kernel, sds(own.shape, BF16), [VMEM] * 3, nbytes=3 << 20)(
+        own, from_below, from_above
+    )
+    from_far = lax.all_to_all(merged, "far", 0, 0, tiled=True)
+    to_plane = call(plane_sum_kernel, sds(fine[2:], F32), [VMEM], nbytes=1 << 20)(from_far)
     from_all = lax.all_to_all(to_plane, ("y", "x"), 0, 0, tiled=True)
-
     total, share = call(
         squares_kernel,
         (sds((deep, cols), F32), sds((chips * nc, 1, cols), F32)),
@@ -311,7 +362,7 @@
     )(where, flags, from_all)
     weight, _ = lax.optimization_barrier((weight, share))
     shares = lax.all_to_all(share, DEV, 0, 0, tiled=True)
-    out = input_grad(g, weight, back, down, 512)
+    out = input_grad(g, weight, back, down, 1024)
     shares, out = lax.optimization_barrier((shares, out))
 
     shape = lambda v: sds(v.shape, v.dtype)
@@ -324,7 +375,7 @@
 
 
 def solution(mesh):
-    sizes = (8, 4, 4, 2)
+    sizes = (4, 2, 4, 4, 2)
     fine = Mesh(mesh.devices.reshape(sizes), DEV)
     split = P(DEV, None)
     return jax.shard_map(

time: 117 us -> 115 us (0.983)
  blocking collectives: 61.6 us -> 42.3 us
  waiting for transfers between devices: 5.04 us -> 18.8 us
  starting transfers between devices: 7.25 us -> 11.5 us
  other arithmetic: 2.72 us -> 0 us
  local copies, waits for them, and re-layouts: 0.04 us -> 2.37 us
    all_to_all x1, blocking collectives: 41.7 us -> 23.1 us  [shards(): from_far = lax.all_to_all(merged, 'far', 0, 0, tiled=True)]
    ppermute x0 -> x2, waiting for transfers between devices: none -> 9.53 us  [shift(): lax.ppermute(value, axis, [(i, (i + by) % size) for i in range(size)])]
    all_gather x1, waiting for transfers between devices: 0.56 us -> 5.35 us  [shards(): weight = lax.all_gather(base_weight, PLANE, axis=0, tiled=True)]
    all_to_all x1, starting transfers between devices: 7.13 us -> 9.31 us  [shards(): shares = lax.all_to_all(share, DEV, 0, 0, tiled=True)]
    convert_element_type x1 -> x0, other arithmetic: 2.13 us -> none  [shards(): to_all = (keep + recv.astype(F32)).astype(BF16)]
    ppermute x0 -> x2, starting transfers between devices: none -> 2.1 us  [shift(): lax.ppermute(value, axis, [(i, (i + by) % size) for i in range(size)])]
    unnamed x16 -> x18, local copies, waits for them, and re-layouts: 0.04 us -> 1.77 us
    pallas_call x1, Pallas kernels: 11.3 us -> 9.93 us  [input_grad(): pl.pallas_call(input_grad_kernel, out_shape=jax.ShapeDtypeStruct((rows, w...]
  transfers between devices with their start and end apart: 3 -> 5, of which waited for: 3 -> 4; matrix products, arithmetic and copies ran while one was open for 2% -> 1% of each run, Pallas kernels for 19% -> 19%
where the time goes in v3:
time: 115 us; the launch traced here: 113 us
  blocking collectives  42.3 us (37%)
  Pallas kernels  23.5 us (20%)
  waiting for transfers between devices  18.8 us (16%)
  between operations  14.2 us (12%)
  starting transfers between devices  11.5 us (10%)
  local copies, waits for them, and re-layouts  2.37 us (2%)
    all_to_all x1, blocking collectives, shards(): from_far = lax.all_to_all(merged, 'far', 0, 0, tiled=True)  23.1 us
    all_to_all x1, blocking collectives, shards(): from_all = lax.all_to_all(to_plane, ('y', 'x'), 0, 0, tiled=True)  19.2 us
    pallas_call x1, Pallas kernels, input_grad(): pl.pallas_call(input_grad_kernel, out_shape=jax.ShapeDtypeStruct((rows, w...  9.93 us
    ppermute x2, waiting for transfers between devices, shift(): lax.ppermute(value, axis, [(i, (i + by) % size) for i in range(size)])  9.53 us
    pallas_call x1, Pallas kernels, shards(): call(grads_kernel, (sds(part, F32), sds(part, BF16), sds((rows, cols), BF...  9.51 us
    all_to_all x1, starting transfers between devices, shards(): shares = lax.all_to_all(share, DEV, 0, 0, tiled=True)  9.31 us
    all_gather x1, waiting for transfers between devices, shards(): weight = lax.all_gather(base_weight, PLANE, axis=0, tiled=True)  5.35 us
    ppermute x1, waiting for transfers between devices, flip(): return lax.ppermute(value, axis, [(i, i ^ bit) for i in range(size)])  3.23 us
  transfers between devices with their start and end apart: 5, of which 4 were waited for; matrix products, arithmetic and copies ran while one was open for 1% of the time, Pallas kernels for 19%

profile of v3, /device:TPU:32, one launch (start us, length us, event | category | flops | bytes accessed | tf_op | source)
XLA Modules:
  0.0 112.7 jit_solution(6974669134778535038)
XLA Ops:
  7.2 0.0 all-gather.2.cloned.1.call-start
  7.2 0.7 all-gather.2.cloned.1.call-update
  7.9 0.6 stack.23.where_ref
  8.5 0.0 copy-start.4
  8.5 9.5 %shard_map.180 = (f32[32,4,40,128]{3,2,1,0:T(8,128)}, bf16[32,4,40,128]{3,2,1,0:T(8,128)(2,1)}, bf16[256,128]{1,0:T(8,128)(2,1)}) custom-call(s32[5]{0:T(128)} %stack.23.where_ref, s32[1,8]{1,0:T(1,128)} %counts_ref.1, bf16[256,8192]{1,0:T(8,128)(2,1)} %tok_hbm.1, bf16[256,1024]{1,0:T(8,128)(2,1)} %g_hbm.3, bf16[8192,128]{1,0:T(8,128)(2,1)} %down_hbm.3, ...), custom_call_target="tpu_custom_call" | custom-call | flops 1073741824 | bytes 12582912 | tf_op jit(solution)/shard_map/pallas_call | solution.py:325
  18.0 0.1 collective-permute-start
  18.1 3.2 %collective-permute-done = bf16[32,4,40,128]{3,2,1,0:T(8,128)(2,1)S(1)} collective-permute-done((bf16[32,4,40,128]{3,2,1,0:T(8,128)(2,1)}, bf16[32,4,40,128]{3,2,1,0:T(8,128)(2,1)S(1)}, u32[]{:S(2)}, u32[]{:S(2)}) %collective-permute-start) | collective-permute-done | bytes 1310752 | tf_op jit(solution)/shard_map/ppermute | solution.py:307
  21.4 0.0 copy-done.4
  21.4 1.7 %copy-done = f32[32,4,40,128]{3,2,1,0:T(8,128)S(1)} copy-done((f32[32,4,40,128]{3,2,1,0:T(8,128)S(1)}, f32[32,4,40,128]{3,2,1,0:T(8,128)}, u32[]{:S(2)}) %copy-start) | copy-done | bytes 2621464
  23.1 0.9 shard_map.181
  24.0 2.0 %collective-permute-start.1 = (bf16[2,16,40,128]{3,2,1,0:T(8,128)(2,1)S(1)}, bf16[2,16,40,128]{3,2,1,0:T(8,128)(2,1)S(1)}, u32[]{:S(2)}, u32[]{:S(2)}) collective-permute-start(bf16[2,16,40,128]{3,2,1,0:T(8,128)(2,1)S(1)} %get-tuple-element.27), channel_id=1, source_target_pairs={{0,32},{32,64},{64,96},{96,128},{128,160},{160,192},{192,224},{224... | collective-permute-start | bytes 983048 | tf_op jit(solution)/shard_map/ppermute | solution.py:303
  26.0 0.1 collective-permute-start.2
  26.1 7.8 %collective-permute-done.1.low_ref = bf16[2,16,40,128]{3,2,1,0:T(8,128)(2,1)S(1)} collective-permute-done((bf16[2,16,40,128]{3,2,1,0:T(8,128)(2,1)S(1)}, bf16[2,16,40,128]{3,2,1,0:T(8,128)(2,1)S(1)}, u32[]{:S(2)}, u32[]{:S(2)}) %collective-permute-start.1) | collective-permute-done | bytes 327712 | tf_op jit(solution)/shard_map/ppermute | solution.py:303
  34.0 1.7 %collective-permute-done.2.high_ref = bf16[2,16,40,128]{3,2,1,0:T(8,128)(2,1)S(1)} collective-permute-done((bf16[2,16,40,128]{3,2,1,0:T(8,128)(2,1)S(1)}, bf16[2,16,40,128]{3,2,1,0:T(8,128)(2,1)S(1)}, u32[]{:S(2)}, u32[]{:S(2)}) %collective-permute-start.2) | collective-permute-done | bytes 327712 | tf_op jit(solution)/shard_map/ppermute | solution.py:303
  35.7 0.1 shard_map.182
  35.8 23.1 %all_to_all.15.parts = bf16[4,16,40,128]{3,2,1,0:T(8,128)(2,1)S(1)} all-to-all(bf16[4,16,40,128]{3,2,1,0:T(8,128)(2,1)S(1)} %shard_map.182), channel_id=1, replica_groups=mesh['far'=4,'near'=2,'y'=4,'x'=4,'c'=2] {'far'}, dimensions={0} | all-to-all | bytes 1310720 | tf_op jit(solution)/shard_map/all_to_all | solution.py:355
  58.9 0.1 shard_map.183
  59.0 19.2 %all_to_all.16.parts = f32[16,40,128]{2,1,0:T(8,128)S(1)} all-to-all(f32[16,40,128]{2,1,0:T(8,128)S(1)} %shard_map.183), channel_id=1, replica_groups=mesh['far'=4,'near'=2,'y'=4,'x'=4,'c'=2] {'y','x'}, dimensions={0} | all-to-all | bytes 655360 | tf_op jit(solution)/shard_map/all_to_all | solution.py:357
  78.2 0.0 copy-done.8
  78.2 1.4 %shard_map.184 = (f32[40,128]{1,0:T(8,128)S(1)}, f32[256,1,128]{2,1,0:T(1,128)}) custom-call(s32[5]{0:T(128)S(1)} %copy-done.4, s32[1,8]{1,0:T(1,128)S(1)} %copy-done.8, f32[16,40,128]{2,1,0:T(8,128)S(1)} %all_to_all.16.parts), custom_call_target="tpu_custom_call" | custom-call | tf_op jit(solution)/shard_map/pallas_call | solution.py:358
  79.6 9.3 %all-to-all-start.2 = ((f32[256,1,128]{2,1,0:T(1,128)}), f32[256,1,128]{2,1,0:T(1,128)S(1)}, u32[]{:S(2)}, u32[]{:S(2)}) async-start(f32[256,1,128]{2,1,0:T(1,128)} %get-tuple-element.29), calls=%async_computation.2 | async-start | bytes 262144 | tf_op jit(solution)/shard_map/all_to_all | solution.py:364
  88.9 5.4 %all-gather.2.cloned.1.call-done.weight_hbm = bf16[8192,1024]{1,0:T(8,128)(2,1)} async-done(((bf16[256,1024]{1,0:T(8,128)(2,1)}), bf16[8192,1024]{1,0:T(8,128)(2,1)}) %all-gather.2.cloned.1.call-update) | async-done | bytes 16777232 | tf_op jit(solution)/shard_map/all_gather | solution.py:319
  94.3 0.0 copy-start.7
  94.3 9.9 %shard_map.185 = bf16[256,8192]{1,0:T(8,128)(2,1)} custom-call(bf16[256,1024]{1,0:T(8,128)(2,1)} %g_hbm.3, bf16[8192,1024]{1,0:T(8,128)(2,1)} %all-gather.2.cloned.1.call-done.weight_hbm, bf16[256,128]{1,0:T(8,128)(2,1)} %get-tuple-element.31.back_hbm, bf16[8192,128]{1,0:T(8,128)(2,1)} %down_hbm.3), custom_call_target="tpu_custom_call" | custom-call | flops 4831838208 | bytes 23068672 | tf_op jit(solution)/shard_map/pallas_call | solution.py:281
  104.2 0.0 all-to-all-done.2.shares_ref
  104.2 0.0 copy-done.1
  104.2 0.0 copy-done.2
  104.3 0.0 copy-done.3
  104.3 0.0 copy-done.5
  104.3 0.0 copy-done.6
  104.3 0.0 copy-done.7
  104.3 1.6 %shard_map.186 = (f32[32,128]{1,0:T(8,128)}, f32[32,128]{1,0:T(8,128)}, f32[32,128]{1,0:T(8,128)}, f32[4,128]{1,0:T(4,128)}, f32[4,128]{1,0:T(4,128)}, /*index=5*/f32[4,128]{1,0:T(4,128)}) custom-call(s32[5]{0:T(128)S(1)} %copy-done.4, f32[40,128]{1,0:T(8,128)S(1)} %get-tuple-element.33.total_ref, f32[256,1,128]{2,1,0:T(1,128)S(1)} %all-to-all-done.2.shares_ref, ...), custom_call_target="tpu_custom_call" | custom-call | tf_op jit(solution)/shard_map/pallas_call | solution.py:369
  (7 shorter events, 0.0 us)
Async XLA Ops:
  7.2 87.1 %all-gather.2.cloned.1.call-start = ((), (), s32[]{:S(2)}) async-start(), calls=%async_computation.3 | async-start | bytes 17301504 | tf_op jit(solution)/shard_map/all_gather | solution.py:319
  8.5 12.9 %copy-start.4 = (s32[5]{0:T(128)S(1)}, s32[5]{0:T(128)}, u32[]{:S(2)}) copy-start(s32[5]{0:T(128)} %stack.23.where_ref) | copy-start | bytes 64
  18.0 3.3 %collective-permute-start = (bf16[32,4,40,128]{3,2,1,0:T(8,128)(2,1)}, bf16[32,4,40,128]{3,2,1,0:T(8,128)(2,1)S(1)}, u32[]{:S(2)}, u32[]{:S(2)}) collective-permute-start(bf16[32,4,40,128]{3,2,1,0:T(8,128)(2,1)} %get-tuple-element.25), channel_id=1, source_target_pairs={{0,1},{1,0},{2,3},{3,2},{4,5},{5,4},{6,7},{7,6},{8,9},{9,8},{10,11... | collective-permute-start | bytes 3932168 | tf_op jit(solution)/shard_map/ppermute | solution.py:307
  21.4 1.7 %copy-start = (f32[32,4,40,128]{3,2,1,0:T(8,128)S(1)}, f32[32,4,40,128]{3,2,1,0:T(8,128)}, u32[]{:S(2)}) copy-start(f32[32,4,40,128]{3,2,1,0:T(8,128)} %get-tuple-element.24) | copy-start | bytes 7864324
  24.0 9.9 %collective-permute-start.1 = (bf16[2,16,40,128]{3,2,1,0:T(8,128)(2,1)S(1)}, bf16[2,16,40,128]{3,2,1,0:T(8,128)(2,1)S(1)}, u32[]{:S(2)}, u32[]{:S(2)}) collective-permute-start(bf16[2,16,40,128]{3,2,1,0:T(8,128)(2,1)S(1)} %get-tuple-element.27), channel_id=1, source_target_pairs={{0,32},{32,64},{64,96},{96,128},{128,160},{160,192},{192,224},{224... | collective-permute-start | bytes 983048 | tf_op jit(solution)/shard_map/ppermute | solution.py:303
  26.0 9.6 %collective-permute-start.2 = (bf16[2,16,40,128]{3,2,1,0:T(8,128)(2,1)S(1)}, bf16[2,16,40,128]{3,2,1,0:T(8,128)(2,1)S(1)}, u32[]{:S(2)}, u32[]{:S(2)}) collective-permute-start(bf16[2,16,40,128]{3,2,1,0:T(8,128)(2,1)S(1)} %get-tuple-element.28), channel_id=1, source_target_pairs={{0,224},{32,0},{64,32},{96,64},{128,96},{160,128},{192,160},{224,1... | collective-permute-start | bytes 983048 | tf_op jit(solution)/shard_map/ppermute | solution.py:303
  35.7 42.5 %copy-start.8 = (s32[1,8]{1,0:T(1,128)S(1)}, s32[1,8]{1,0:T(1,128)}, u32[]{:S(2)}) copy-start(s32[1,8]{1,0:T(1,128)} %flags_ref.1) | copy-start | bytes 100
  79.6 24.6 %all-to-all-start.2 = ((f32[256,1,128]{2,1,0:T(1,128)}), f32[256,1,128]{2,1,0:T(1,128)S(1)}, u32[]{:S(2)}, u32[]{:S(2)}) async-start(f32[256,1,128]{2,1,0:T(1,128)} %get-tuple-element.29), calls=%async_computation.2 | async-start | bytes 262144 | tf_op jit(solution)/shard_map/all_to_all | solution.py:364
  94.3 10.0 %copy-start.1 = (f32[32,128]{1,0:T(8,128)S(1)}, f32[32,128]{1,0:T(8,128)}, u32[]{:S(2)}) copy-start(f32[32,128]{1,0:T(8,128)} %master_a.1) | copy-start | bytes 49156
  94.3 10.0 %copy-start.2 = (f32[32,128]{1,0:T(8,128)S(1)}, f32[32,128]{1,0:T(8,128)}, u32[]{:S(2)}) copy-start(f32[32,128]{1,0:T(8,128)} %moment_a.1) | copy-start | bytes 49156
  94.3 10.0 %copy-start.3 = (f32[32,128]{1,0:T(8,128)S(1)}, f32[32,128]{1,0:T(8,128)}, u32[]{:S(2)}) copy-start(f32[32,128]{1,0:T(8,128)} %second_a.1) | copy-start | bytes 49156
  94.3 10.0 %copy-start.5 = (f32[4,128]{1,0:T(4,128)S(1)}, f32[4,128]{1,0:T(4,128)}, u32[]{:S(2)}) copy-start(f32[4,128]{1,0:T(4,128)} %master_b.1) | copy-start | bytes 6148
  94.3 10.0 %copy-start.6 = (f32[4,128]{1,0:T(4,128)S(1)}, f32[4,128]{1,0:T(4,128)}, u32[]{:S(2)}) copy-start(f32[4,128]{1,0:T(4,128)} %moment_b.1) | copy-start | bytes 6148
  94.3 10.0 %copy-start.7 = (f32[4,128]{1,0:T(4,128)S(1)}, f32[4,128]{1,0:T(4,128)}, u32[]{:S(2)}) copy-start(f32[4,128]{1,0:T(4,128)} %second_b.1) | copy-start | bytes 6148
Sparse Core Ops, SparseCore 0:
  10.6 83.6 all-gather.1

commit v4 on v3

--- a/solution.py
+++ b/solution.py
@@ -39,7 +39,7 @@
 
 
 def grads_kernel(
-    where_ref, counts_ref, tok_hbm, g_hbm, down_hbm, up_hbm,
+    nx, where_ref, counts_ref, tok_hbm, g_hbm, down_hbm, up_hbm,
     keep_hbm, send_hbm, back_ref,
     tok, g, down, up, keep_ref, send_ref, sems, small_sems, out_sems,
 ):
@@ -50,7 +50,7 @@
     rank = cols // adapters
     tiles = sems.shape[0]
     tile = width // tiles
-    blocks, nx = keep_ref.shape[:2]
+    blocks = keep_ref.shape[0]
     block = width // blocks
     half = block // nx // 2
     few = kv // blocks // nx
@@ -96,9 +96,9 @@
     for s in range(kv // block):
         r = lax.dot_general(
             g[:, s * block : (s + 1) * block], low, CONTRACT_FIRST, preferred_element_type=F32
-        ).reshape(group, nx, few, cols)
-        keep_ref[s * group : (s + 1) * group, :, half:] = r
-        send_ref[s * group : (s + 1) * group, :, half:] = r.astype(BF16)
+        ).reshape(group, nx * few, cols)
+        keep_ref[s * group : (s + 1) * group, nx * half :] = r
+        send_ref[s * group : (s + 1) * group, nx * half :] = r.astype(BF16)
     per = blocks // tiles
     stores = []
     for t in range(tiles):
@@ -107,8 +107,10 @@
                 tok[:, b * block : (b + 1) * block], back, CONTRACT_FIRST,
                 preferred_element_type=F32,
             ).reshape(nx, 2, half, cols)
-            keep_ref[b, :, :half] = jnp.where(first, r[:, 0], r[:, 1])
-            send_ref[b, :, :half] = jnp.where(first, r[:, 1], r[:, 0]).astype(BF16)
+            ours = jnp.where(first, r[:, 0], r[:, 1]).reshape(nx * half, cols)
+            other = jnp.where(first, r[:, 1], r[:, 0]).reshape(nx * half, cols)
+            keep_ref[b, : nx * half] = ours
+            send_ref[b, : nx * half] = other.astype(BF16)
         span = pl.ds(t * per, per)
         for i, (src, dst) in enumerate(((send_ref, send_hbm), (keep_ref, keep_hbm))):
             stores.append(pltpu.make_async_copy(src.at[span], dst.at[span], out_sems.at[t, i]))
@@ -156,17 +158,33 @@
     )(where, keep, recv)
 
 
-def merge_kernel(own_ref, low_ref, high_ref, out_ref):
+def merge_kernel(where_ref, own_ref, low_ref, high_ref, out_ref, mine_ref):
     half = low_ref.shape[0]
-    out_ref[:half] = (own_ref[:half] + low_ref[...].astype(F32)).astype(BF16)
-    out_ref[half:] = (own_ref[half:] + high_ref[...].astype(F32)).astype(BF16)
-
-
-def plane_sum_kernel(parts, out):
-    total = parts[0].astype(F32)
-    for z in range(1, parts.shape[0]):
-        total = total + parts[z].astype(F32)
-    out[...] = total
+    far = where_ref[0]
+    for i in range(2 * half):
+        other = low_ref[i] if i < half else high_ref[i - half]
+        total = own_ref[i] + other.astype(F32)
+        out_ref[i] = total.astype(BF16)
+
+        @pl.when(far == i)
+        def _():
+            mine_ref[...] = total
+
+
+def plane_sum_kernel(where_ref, mine_ref, parts, out):
+    ny = parts.shape[1]
+    chips, deep = out.shape[:2]
+    nx = chips // ny
+    few = deep // 5
+    many = deep - few
+    total = mine_ref[...]
+    for z in range(parts.shape[0]):
+        total = total + jnp.where(where_ref[0] == z, 0.0, parts[z].astype(F32))
+    for y in range(ny):
+        for x in range(nx):
+            at = nx * many + x * few
+            out[y * nx + x, :many] = total[y, x * many : (x + 1) * many]
+            out[y * nx + x, many:] = total[y, at : at + few]
 
 
 def squares_kernel(where_ref, flags_ref, parts, total_ref, share_ref):
@@ -320,10 +338,10 @@
 
     blocks = nz * ny
     deep = width // blocks // nx // nc + kv // blocks // nx
-    part = (blocks, nx, deep, cols)
+    part = (blocks, nx * deep, cols)
     tiles = 8
     keep, send, back = call(
-        grads_kernel,
+        functools.partial(grads_kernel, nx),
         (sds(part, F32), sds(part, BF16), sds((rows, cols), BF16)),
         [SMEM, SMEM, HBM, HBM, HBM, HBM],
         [
@@ -345,15 +363,23 @@
 
     recv = flip(send, "c", nc, 1)
     chips = nz * ny * nx
-    fine = (nf, nn, ny * nx, deep, cols)
+    fine = (nf, nn, ny, nx * deep, cols)
     own, up, low = split(where, keep.reshape(fine), recv.reshape(fine))
     z_axes = ("far", "near")
     from_below, from_above = shift(up, z_axes, nz, 1), shift(low, z_axes, nz, -1)
-    merged = call(merge_kernel, sds(own.shape, BF16), [VMEM] * 3, nbytes=3 << 20)(
-        own, from_below, from_above
-    )
+    merged, mine = call(
+        merge_kernel,
+        (sds(own.shape, BF16), sds(own.shape[1:], F32)),
+        [SMEM] + [VMEM] * 3,
+        nbytes=3 << 20,
+    )(where, own, from_below, from_above)
     from_far = lax.all_to_all(merged, "far", 0, 0, tiled=True)
-    to_plane = call(plane_sum_kernel, sds(fine[2:], F32), [VMEM], nbytes=1 << 20)(from_far)
+    to_plane = call(
+        plane_sum_kernel,
+        sds((ny * nx, deep, cols), F32),
+        [SMEM, VMEM, VMEM],
+        nbytes=1 << 20,
+    )(where, mine, from_far)
     from_all = lax.all_to_all(to_plane, ("y", "x"), 0, 0, tiled=True)
     total, share = call(
         squares_kernel,

time: 115 us -> 114 us (level)
  waiting for transfers between devices: 18.8 us -> 17.6 us
    all_gather x1, waiting for transfers between devices: 5.35 us -> 4.17 us  [shards(): weight = lax.all_gather(base_weight, PLANE, axis=0, tiled=True)]
  transfers between devices with their start and end apart: 5 -> 5, of which waited for: 4 -> 4; matrix products, arithmetic and copies ran while one was open for 1% -> 1% of each run, Pallas kernels for 19% -> 20%
where the time goes in v4:
time: 114 us; the launch traced here: 113 us
  blocking collectives  42.3 us (37%)
  Pallas kernels  24.6 us (22%)
  waiting for transfers between devices  17.6 us (15%)
  between operations  14.2 us (12%)
  starting transfers between devices  11.5 us (10%)
  local copies, waits for them, and re-layouts  2.37 us (2%)
    all_to_all x1, blocking collectives, shards(): from_far = lax.all_to_all(merged, 'far', 0, 0, tiled=True)  23.1 us
    all_to_all x1, blocking collectives, shards(): from_all = lax.all_to_all(to_plane, ('y', 'x'), 0, 0, tiled=True)  19.2 us
    pallas_call x1, Pallas kernels, input_grad(): pl.pallas_call(input_grad_kernel, out_shape=jax.ShapeDtypeStruct((rows, w...  9.93 us
    ppermute x2, waiting for transfers between devices, shift(): lax.ppermute(value, axis, [(i, (i + by) % size) for i in range(size)])  9.53 us
    pallas_call x1, Pallas kernels, shards(): call(functools.partial(grads_kernel, nx), (sds(part, F32), sds(part, BF16...  9.5 us
    all_to_all x1, starting transfers between devices, shards(): shares = lax.all_to_all(share, DEV, 0, 0, tiled=True)  9.29 us
    all_gather x1, waiting for transfers between devices, shards(): weight = lax.all_gather(base_weight, PLANE, axis=0, tiled=True)  4.17 us
    ppermute x1, waiting for transfers between devices, flip(): return lax.ppermute(value, axis, [(i, i ^ bit) for i in range(size)])  3.23 us
  transfers between devices with their start and end apart: 5, of which 4 were waited for; matrix products, arithmetic and copies ran while one was open for 1% of the time, Pallas kernels for 20%

profile of v4, /device:TPU:32, one launch (start us, length us, event | category | flops | bytes accessed | tf_op | source)
XLA Modules:
  0.0 112.6 jit_solution(467426731462598949)
XLA Ops:
  7.2 0.0 all-gather.2.cloned.1.call-start
  7.2 0.7 all-gather.2.cloned.1.call-update
  7.9 0.6 stack.23.where_ref
  8.5 0.0 copy-start.1
  8.5 9.5 %shard_map.180 = (f32[32,160,128]{2,1,0:T(8,128)}, bf16[32,160,128]{2,1,0:T(8,128)(2,1)}, bf16[256,128]{1,0:T(8,128)(2,1)}) custom-call(s32[5]{0:T(128)} %stack.23.where_ref, s32[1,8]{1,0:T(1,128)} %counts_ref.1, bf16[256,8192]{1,0:T(8,128)(2,1)} %tok_hbm.1, bf16[256,1024]{1,0:T(8,128)(2,1)} %g_hbm.3, bf16[8192,128]{1,0:T(8,128)(2,1)} %down_hbm.3, ...), custom_call_target="tpu_custom_call" | custom-call | flops 1073741824 | bytes 12582912 | tf_op jit(solution)/shard_map/pallas_call | solution.py:343
  18.0 0.1 collective-permute-start
  18.1 3.2 %collective-permute-done = bf16[32,160,128]{2,1,0:T(8,128)(2,1)S(1)} collective-permute-done((bf16[32,160,128]{2,1,0:T(8,128)(2,1)}, bf16[32,160,128]{2,1,0:T(8,128)(2,1)S(1)}, u32[]{:S(2)}, u32[]{:S(2)}) %collective-permute-start) | collective-permute-done | bytes 1310752 | tf_op jit(solution)/shard_map/ppermute | solution.py:325
  21.4 0.0 copy-done.1
  21.4 1.7 %copy-done = f32[32,160,128]{2,1,0:T(8,128)S(1)} copy-done((f32[32,160,128]{2,1,0:T(8,128)S(1)}, f32[32,160,128]{2,1,0:T(8,128)}, u32[]{:S(2)}) %copy-start) | copy-done | bytes 2621464
  23.1 0.9 shard_map.181
  24.0 2.0 %collective-permute-start.1 = (bf16[2,4,160,128]{3,2,1,0:T(8,128)(2,1)S(1)}, bf16[2,4,160,128]{3,2,1,0:T(8,128)(2,1)S(1)}, u32[]{:S(2)}, u32[]{:S(2)}) collective-permute-start(bf16[2,4,160,128]{3,2,1,0:T(8,128)(2,1)S(1)} %get-tuple-element.29), channel_id=1, source_target_pairs={{0,32},{32,64},{64,96},{96,128},{128,160},{160,192},{192,224},{224... | collective-permute-start | bytes 983048 | tf_op jit(solution)/shard_map/ppermute | solution.py:321
  26.0 0.1 collective-permute-start.2
  26.1 7.8 %collective-permute-done.1.low_ref = bf16[2,4,160,128]{3,2,1,0:T(8,128)(2,1)S(1)} collective-permute-done((bf16[2,4,160,128]{3,2,1,0:T(8,128)(2,1)S(1)}, bf16[2,4,160,128]{3,2,1,0:T(8,128)(2,1)S(1)}, u32[]{:S(2)}, u32[]{:S(2)}) %collective-permute-start.1) | collective-permute-done | bytes 327712 | tf_op jit(solution)/shard_map/ppermute | solution.py:321
  34.0 1.7 %collective-permute-done.2.high_ref = bf16[2,4,160,128]{3,2,1,0:T(8,128)(2,1)S(1)} collective-permute-done((bf16[2,4,160,128]{3,2,1,0:T(8,128)(2,1)S(1)}, bf16[2,4,160,128]{3,2,1,0:T(8,128)(2,1)S(1)}, u32[]{:S(2)}, u32[]{:S(2)}) %collective-permute-start.2) | collective-permute-done | bytes 327712 | tf_op jit(solution)/shard_map/ppermute | solution.py:321
  35.7 0.7 shard_map.182
  36.4 23.1 %all_to_all.15.parts = bf16[4,4,160,128]{3,2,1,0:T(8,128)(2,1)S(1)} all-to-all(bf16[4,4,160,128]{3,2,1,0:T(8,128)(2,1)S(1)} %get-tuple-element.32), channel_id=1, replica_groups=mesh['far'=4,'near'=2,'y'=4,'x'=4,'c'=2] {'far'}, dimensions={0} | all-to-all | bytes 1310720 | tf_op jit(solution)/shard_map/all_to_all | solution.py:376
  59.4 0.7 shard_map.183
  60.1 19.2 %all_to_all.16.parts = f32[16,40,128]{2,1,0:T(8,128)S(1)} all-to-all(f32[16,40,128]{2,1,0:T(8,128)S(1)} %shard_map.183), channel_id=1, replica_groups=mesh['far'=4,'near'=2,'y'=4,'x'=4,'c'=2] {'y','x'}, dimensions={0} | all-to-all | bytes 655360 | tf_op jit(solution)/shard_map/all_to_all | solution.py:383
  79.4 0.0 copy-done.8
  79.4 1.4 %shard_map.184 = (f32[40,128]{1,0:T(8,128)S(1)}, f32[256,1,128]{2,1,0:T(1,128)}) custom-call(s32[5]{0:T(128)S(1)} %copy-done.1, s32[1,8]{1,0:T(1,128)S(1)} %copy-done.8, f32[16,40,128]{2,1,0:T(8,128)S(1)} %all_to_all.16.parts), custom_call_target="tpu_custom_call" | custom-call | tf_op jit(solution)/shard_map/pallas_call | solution.py:384
  80.7 9.3 %all-to-all-start.2 = ((f32[256,1,128]{2,1,0:T(1,128)}), f32[256,1,128]{2,1,0:T(1,128)S(1)}, u32[]{:S(2)}, u32[]{:S(2)}) async-start(f32[256,1,128]{2,1,0:T(1,128)} %get-tuple-element.33), calls=%async_computation.2 | async-start | bytes 262144 | tf_op jit(solution)/shard_map/all_to_all | solution.py:390
  90.0 4.2 %all-gather.2.cloned.1.call-done.weight_hbm = bf16[8192,1024]{1,0:T(8,128)(2,1)} async-done(((bf16[256,1024]{1,0:T(8,128)(2,1)}), bf16[8192,1024]{1,0:T(8,128)(2,1)}) %all-gather.2.cloned.1.call-update) | async-done | bytes 16777232 | tf_op jit(solution)/shard_map/all_gather | solution.py:337
  94.2 0.0 copy-start.7
  94.2 9.9 %shard_map.185 = bf16[256,8192]{1,0:T(8,128)(2,1)} custom-call(bf16[256,1024]{1,0:T(8,128)(2,1)} %g_hbm.3, bf16[8192,1024]{1,0:T(8,128)(2,1)} %all-gather.2.cloned.1.call-done.weight_hbm, bf16[256,128]{1,0:T(8,128)(2,1)} %get-tuple-element.35.back_hbm, bf16[8192,128]{1,0:T(8,128)(2,1)} %down_hbm.3), custom_call_target="tpu_custom_call" | custom-call | flops 4831838208 | bytes 23068672 | tf_op jit(solution)/shard_map/pallas_call | solution.py:299
  104.2 0.0 all-to-all-done.2.shares_ref
  104.2 0.0 copy-done.2
  104.2 0.0 copy-done.3
  104.2 0.0 copy-done.4
  104.2 0.0 copy-done.5
  104.2 0.0 copy-done.6
  104.2 0.0 copy-done.7
  104.2 1.5 %shard_map.186 = (f32[32,128]{1,0:T(8,128)}, f32[32,128]{1,0:T(8,128)}, f32[32,128]{1,0:T(8,128)}, f32[4,128]{1,0:T(4,128)}, f32[4,128]{1,0:T(4,128)}, /*index=5*/f32[4,128]{1,0:T(4,128)}) custom-call(s32[5]{0:T(128)S(1)} %copy-done.1, f32[40,128]{1,0:T(8,128)S(1)} %get-tuple-element.37.total_ref, f32[256,1,128]{2,1,0:T(1,128)S(1)} %all-to-all-done.2.shares_ref, ...), custom_call_target="tpu_custom_call" | custom-call | tf_op jit(solution)/shard_map/pallas_call | solution.py:395
  (7 shorter events, 0.0 us)
Async XLA Ops:
  7.2 87.0 %all-gather.2.cloned.1.call-start = ((), (), s32[]{:S(2)}) async-start(), calls=%async_computation.3 | async-start | bytes 17301504 | tf_op jit(solution)/shard_map/all_gather | solution.py:337
  8.5 12.8 %copy-start.1 = (s32[5]{0:T(128)S(1)}, s32[5]{0:T(128)}, u32[]{:S(2)}) copy-start(s32[5]{0:T(128)} %stack.23.where_ref) | copy-start | bytes 64
  18.0 3.3 %collective-permute-start = (bf16[32,160,128]{2,1,0:T(8,128)(2,1)}, bf16[32,160,128]{2,1,0:T(8,128)(2,1)S(1)}, u32[]{:S(2)}, u32[]{:S(2)}) collective-permute-start(bf16[32,160,128]{2,1,0:T(8,128)(2,1)} %get-tuple-element.27), channel_id=1, source_target_pairs={{0,1},{1,0},{2,3},{3,2},{4,5},{5,4},{6,7},{7,6},{8,9},{9,8},{10,11... | collective-permute-start | bytes 3932168 | tf_op jit(solution)/shard_map/ppermute | solution.py:325
  21.4 1.7 %copy-start = (f32[32,160,128]{2,1,0:T(8,128)S(1)}, f32[32,160,128]{2,1,0:T(8,128)}, u32[]{:S(2)}) copy-start(f32[32,160,128]{2,1,0:T(8,128)} %get-tuple-element.26) | copy-start | bytes 7864324
  24.0 9.9 %collective-permute-start.1 = (bf16[2,4,160,128]{3,2,1,0:T(8,128)(2,1)S(1)}, bf16[2,4,160,128]{3,2,1,0:T(8,128)(2,1)S(1)}, u32[]{:S(2)}, u32[]{:S(2)}) collective-permute-start(bf16[2,4,160,128]{3,2,1,0:T(8,128)(2,1)S(1)} %get-tuple-element.29), channel_id=1, source_target_pairs={{0,32},{32,64},{64,96},{96,128},{128,160},{160,192},{192,224},{224... | collective-permute-start | bytes 983048 | tf_op jit(solution)/shard_map/ppermute | solution.py:321
  26.0 9.6 %collective-permute-start.2 = (bf16[2,4,160,128]{3,2,1,0:T(8,128)(2,1)S(1)}, bf16[2,4,160,128]{3,2,1,0:T(8,128)(2,1)S(1)}, u32[]{:S(2)}, u32[]{:S(2)}) collective-permute-start(bf16[2,4,160,128]{3,2,1,0:T(8,128)(2,1)S(1)} %get-tuple-element.30), channel_id=1, source_target_pairs={{0,224},{32,0},{64,32},{96,64},{128,96},{160,128},{192,160},{224,1... | collective-permute-start | bytes 983048 | tf_op jit(solution)/shard_map/ppermute | solution.py:321
  35.7 43.7 %copy-start.8 = (s32[1,8]{1,0:T(1,128)S(1)}, s32[1,8]{1,0:T(1,128)}, u32[]{:S(2)}) copy-start(s32[1,8]{1,0:T(1,128)} %flags_ref.1) | copy-start | bytes 100
  80.7 23.4 %all-to-all-start.2 = ((f32[256,1,128]{2,1,0:T(1,128)}), f32[256,1,128]{2,1,0:T(1,128)S(1)}, u32[]{:S(2)}, u32[]{:S(2)}) async-start(f32[256,1,128]{2,1,0:T(1,128)} %get-tuple-element.33), calls=%async_computation.2 | async-start | bytes 262144 | tf_op jit(solution)/shard_map/all_to_all | solution.py:390
  94.2 10.0 %copy-start.2 = (f32[32,128]{1,0:T(8,128)S(1)}, f32[32,128]{1,0:T(8,128)}, u32[]{:S(2)}) copy-start(f32[32,128]{1,0:T(8,128)} %master_a.1) | copy-start | bytes 49156
  94.2 10.0 %copy-start.3 = (f32[32,128]{1,0:T(8,128)S(1)}, f32[32,128]{1,0:T(8,128)}, u32[]{:S(2)}) copy-start(f32[32,128]{1,0:T(8,128)} %moment_a.1) | copy-start | bytes 49156
  94.2 10.0 %copy-start.4 = (f32[32,128]{1,0:T(8,128)S(1)}, f32[32,128]{1,0:T(8,128)}, u32[]{:S(2)}) copy-start(f32[32,128]{1,0:T(8,128)} %second_a.1) | copy-start | bytes 49156
  94.2 10.0 %copy-start.5 = (f32[4,128]{1,0:T(4,128)S(1)}, f32[4,128]{1,0:T(4,128)}, u32[]{:S(2)}) copy-start(f32[4,128]{1,0:T(4,128)} %master_b.1) | copy-start | bytes 6148
  94.2 10.0 %copy-start.6 = (f32[4,128]{1,0:T(4,128)S(1)}, f32[4,128]{1,0:T(4,128)}, u32[]{:S(2)}) copy-start(f32[4,128]{1,0:T(4,128)} %moment_b.1) | copy-start | bytes 6148
  94.2 10.0 %copy-start.7 = (f32[4,128]{1,0:T(4,128)S(1)}, f32[4,128]{1,0:T(4,128)}, u32[]{:S(2)}) copy-start(f32[4,128]{1,0:T(4,128)} %second_b.1) | copy-start | bytes 6148
Sparse Core Ops, SparseCore 0:
  10.6 83.6 all-gather.1

commit v5 on v4

--- a/solution.py
+++ b/solution.py
@@ -308,7 +308,7 @@
             pltpu.SemaphoreType.DMA((2 * chunks + 2,)),
             pltpu.SemaphoreType.DMA((chunks,)),
         ],
-        compiler_params=pltpu.CompilerParams(vmem_limit_bytes=60 << 20),
+        compiler_params=pltpu.CompilerParams(vmem_limit_bytes=52 << 20),
         cost_estimate=pl.CostEstimate(
             flops=2 * rows * width * (kv + cols),
             bytes_accessed=2 * width * (kv + cols + rows),

time: 114 us -> 114 us (level)
  no operation moved by 1% of the time
where the time goes in v5:
time: 114 us; the launch traced here: 112 us
  blocking collectives  42.3 us (37%)
  Pallas kernels  24.4 us (21%)
  waiting for transfers between devices  17.6 us (15%)
  between operations  14.2 us (12%)
  starting transfers between devices  11.5 us (10%)
  local copies, waits for them, and re-layouts  2.39 us (2%)
    all_to_all x1, blocking collectives, shards(): from_far = lax.all_to_all(merged, 'far', 0, 0, tiled=True)  23.1 us
    all_to_all x1, blocking collectives, shards(): from_all = lax.all_to_all(to_plane, ('y', 'x'), 0, 0, tiled=True)  19.3 us
    pallas_call x1, Pallas kernels, input_grad(): pl.pallas_call(input_grad_kernel, out_shape=jax.ShapeDtypeStruct((rows, w...  9.73 us
    ppermute x2, waiting for transfers between devices, shift(): lax.ppermute(value, axis, [(i, (i + by) % size) for i in range(size)])  9.53 us
    pallas_call x1, Pallas kernels, shards(): call(functools.partial(grads_kernel, nx), (sds(part, F32), sds(part, BF16...  9.5 us
    all_to_all x1, starting transfers between devices, shards(): shares = lax.all_to_all(share, DEV, 0, 0, tiled=True)  9.26 us
    all_gather x1, waiting for transfers between devices, shards(): weight = lax.all_gather(base_weight, PLANE, axis=0, tiled=True)  4.2 us
    ppermute x1, waiting for transfers between devices, flip(): return lax.ppermute(value, axis, [(i, i ^ bit) for i in range(size)])  3.23 us
  transfers between devices with their start and end apart: 5, of which 4 were waited for; matrix products, arithmetic and copies ran while one was open for 1% of the time, Pallas kernels for 20%

profile of v5, /device:TPU:32, one launch (start us, length us, event | category | flops | bytes accessed | tf_op | source)
XLA Modules:
  0.0 112.5 jit_solution(1036973160981165409)
XLA Ops:
  7.2 0.0 all-gather.2.cloned.1.call-start
  7.2 0.7 all-gather.2.cloned.1.call-update
  7.9 0.6 stack.23.where_ref
  8.5 9.5 %shard_map.180 = (f32[32,160,128]{2,1,0:T(8,128)}, bf16[32,160,128]{2,1,0:T(8,128)(2,1)}, bf16[256,128]{1,0:T(8,128)(2,1)}) custom-call(s32[5]{0:T(128)} %stack.23.where_ref, s32[1,8]{1,0:T(1,128)} %counts_ref.1, bf16[256,8192]{1,0:T(8,128)(2,1)} %tok_hbm.1, bf16[256,1024]{1,0:T(8,128)(2,1)} %g_hbm.3, bf16[8192,128]{1,0:T(8,128)(2,1)} %down_hbm.3, ...), custom_call_target="tpu_custom_call" | custom-call | flops 1073741824 | bytes 12582912 | tf_op jit(solution)/shard_map/pallas_call | solution.py:343
  18.0 0.1 collective-permute-start
  18.1 3.2 %collective-permute-done = bf16[32,160,128]{2,1,0:T(8,128)(2,1)S(1)} collective-permute-done((bf16[32,160,128]{2,1,0:T(8,128)(2,1)}, bf16[32,160,128]{2,1,0:T(8,128)(2,1)S(1)}, u32[]{:S(2)}, u32[]{:S(2)}) %collective-permute-start) | collective-permute-done | bytes 1310752 | tf_op jit(solution)/shard_map/ppermute | solution.py:325
  21.4 0.0 copy-done.3
  21.4 1.7 %copy-done = f32[32,160,128]{2,1,0:T(8,128)S(1)} copy-done((f32[32,160,128]{2,1,0:T(8,128)S(1)}, f32[32,160,128]{2,1,0:T(8,128)}, u32[]{:S(2)}) %copy-start) | copy-done | bytes 2621464
  23.1 0.9 shard_map.181
  24.0 2.0 %collective-permute-start.1 = (bf16[2,4,160,128]{3,2,1,0:T(8,128)(2,1)S(1)}, bf16[2,4,160,128]{3,2,1,0:T(8,128)(2,1)S(1)}, u32[]{:S(2)}, u32[]{:S(2)}) collective-permute-start(bf16[2,4,160,128]{3,2,1,0:T(8,128)(2,1)S(1)} %get-tuple-element.29), channel_id=1, source_target_pairs={{0,32},{32,64},{64,96},{96,128},{128,160},{160,192},{192,224},{224... | collective-permute-start | bytes 983048 | tf_op jit(solution)/shard_map/ppermute | solution.py:321
  26.0 0.1 collective-permute-start.2
  26.1 7.8 %collective-permute-done.1.low_ref = bf16[2,4,160,128]{3,2,1,0:T(8,128)(2,1)S(1)} collective-permute-done((bf16[2,4,160,128]{3,2,1,0:T(8,128)(2,1)S(1)}, bf16[2,4,160,128]{3,2,1,0:T(8,128)(2,1)S(1)}, u32[]{:S(2)}, u32[]{:S(2)}) %collective-permute-start.1) | collective-permute-done | bytes 327712 | tf_op jit(solution)/shard_map/ppermute | solution.py:321
  34.0 1.7 %collective-permute-done.2.high_ref = bf16[2,4,160,128]{3,2,1,0:T(8,128)(2,1)S(1)} collective-permute-done((bf16[2,4,160,128]{3,2,1,0:T(8,128)(2,1)S(1)}, bf16[2,4,160,128]{3,2,1,0:T(8,128)(2,1)S(1)}, u32[]{:S(2)}, u32[]{:S(2)}) %collective-permute-start.2) | collective-permute-done | bytes 327712 | tf_op jit(solution)/shard_map/ppermute | solution.py:321
  35.7 0.7 shard_map.182
  36.4 23.1 %all_to_all.15.parts = bf16[4,4,160,128]{3,2,1,0:T(8,128)(2,1)S(1)} all-to-all(bf16[4,4,160,128]{3,2,1,0:T(8,128)(2,1)S(1)} %get-tuple-element.32), channel_id=1, replica_groups=mesh['far'=4,'near'=2,'y'=4,'x'=4,'c'=2] {'far'}, dimensions={0} | all-to-all | bytes 1310720 | tf_op jit(solution)/shard_map/all_to_all | solution.py:376
  59.4 0.7 shard_map.183
  60.1 19.3 %all_to_all.16.parts = f32[16,40,128]{2,1,0:T(8,128)S(1)} all-to-all(f32[16,40,128]{2,1,0:T(8,128)S(1)} %shard_map.183), channel_id=1, replica_groups=mesh['far'=4,'near'=2,'y'=4,'x'=4,'c'=2] {'y','x'}, dimensions={0} | all-to-all | bytes 655360 | tf_op jit(solution)/shard_map/all_to_all | solution.py:383
  79.4 1.4 %shard_map.184 = (f32[40,128]{1,0:T(8,128)S(1)}, f32[256,1,128]{2,1,0:T(1,128)}) custom-call(s32[5]{0:T(128)S(1)} %copy-done.3, s32[1,8]{1,0:T(1,128)S(1)} %copy-done.10, f32[16,40,128]{2,1,0:T(8,128)S(1)} %all_to_all.16.parts), custom_call_target="tpu_custom_call" | custom-call | tf_op jit(solution)/shard_map/pallas_call | solution.py:384
  80.7 9.3 %all-to-all-start.2 = ((f32[256,1,128]{2,1,0:T(1,128)}), f32[256,1,128]{2,1,0:T(1,128)S(1)}, u32[]{:S(2)}, u32[]{:S(2)}) async-start(f32[256,1,128]{2,1,0:T(1,128)} %get-tuple-element.33), calls=%async_computation.2 | async-start | bytes 262144 | tf_op jit(solution)/shard_map/all_to_all | solution.py:390
  90.0 4.2 %all-gather.2.cloned.1.call-done.weight_hbm = bf16[8192,1024]{1,0:T(8,128)(2,1)} async-done(((bf16[256,1024]{1,0:T(8,128)(2,1)}), bf16[8192,1024]{1,0:T(8,128)(2,1)}) %all-gather.2.cloned.1.call-update) | async-done | bytes 16777232 | tf_op jit(solution)/shard_map/all_gather | solution.py:337
  94.2 0.0 copy-done.2
  94.2 0.0 copy-start.6
  94.2 0.0 copy-start.7
  94.2 0.0 copy-start.8
  94.2 0.0 copy-start.9
  94.3 9.7 %shard_map.185 = bf16[256,8192]{1,0:T(8,128)(2,1)} custom-call(bf16[256,1024]{1,0:T(8,128)(2,1)S(1)} %copy-done.1, bf16[8192,1024]{1,0:T(8,128)(2,1)} %all-gather.2.cloned.1.call-done.weight_hbm, bf16[256,128]{1,0:T(8,128)(2,1)S(1)} %copy-done.2, bf16[8192,128]{1,0:T(8,128)(2,1)} %down_hbm.3), custom_call_target="tpu_custom_call" | custom-call | flops 4831838208 | bytes 23068672 | tf_op jit(solution)/shard_map/pallas_call | solution.py:299
  104.0 0.0 all-to-all-done.2.shares_ref
  104.0 0.0 copy-done.4
  104.0 0.0 copy-done.5
  104.0 0.0 copy-done.6
  104.0 0.0 copy-done.7
  104.1 1.5 %shard_map.186 = (f32[32,128]{1,0:T(8,128)}, f32[32,128]{1,0:T(8,128)}, f32[32,128]{1,0:T(8,128)}, f32[4,128]{1,0:T(4,128)}, f32[4,128]{1,0:T(4,128)}, /*index=5*/f32[4,128]{1,0:T(4,128)}) custom-call(s32[5]{0:T(128)S(1)} %copy-done.3, f32[40,128]{1,0:T(8,128)S(1)} %get-tuple-element.37.total_ref, f32[256,1,128]{2,1,0:T(1,128)S(1)} %all-to-all-done.2.shares_ref, ...), custom_call_target="tpu_custom_call" | custom-call | tf_op jit(solution)/shard_map/pallas_call | solution.py:395
  (11 shorter events, 0.0 us)
Async XLA Ops:
  7.2 87.0 %all-gather.2.cloned.1.call-start = ((), (), s32[]{:S(2)}) async-start(), calls=%async_computation.3 | async-start | bytes 17301504 | tf_op jit(solution)/shard_map/all_gather | solution.py:337
  8.5 12.8 %copy-start.3 = (s32[5]{0:T(128)S(1)}, s32[5]{0:T(128)}, u32[]{:S(2)}) copy-start(s32[5]{0:T(128)} %stack.23.where_ref) | copy-start | bytes 64
  18.0 3.3 %collective-permute-start = (bf16[32,160,128]{2,1,0:T(8,128)(2,1)}, bf16[32,160,128]{2,1,0:T(8,128)(2,1)S(1)}, u32[]{:S(2)}, u32[]{:S(2)}) collective-permute-start(bf16[32,160,128]{2,1,0:T(8,128)(2,1)} %get-tuple-element.27), channel_id=1, source_target_pairs={{0,1},{1,0},{2,3},{3,2},{4,5},{5,4},{6,7},{7,6},{8,9},{9,8},{10,11... | collective-permute-start | bytes 3932168 | tf_op jit(solution)/shard_map/ppermute | solution.py:325
  21.4 1.7 %copy-start = (f32[32,160,128]{2,1,0:T(8,128)S(1)}, f32[32,160,128]{2,1,0:T(8,128)}, u32[]{:S(2)}) copy-start(f32[32,160,128]{2,1,0:T(8,128)} %get-tuple-element.26) | copy-start | bytes 7864324
  24.0 9.9 %collective-permute-start.1 = (bf16[2,4,160,128]{3,2,1,0:T(8,128)(2,1)S(1)}, bf16[2,4,160,128]{3,2,1,0:T(8,128)(2,1)S(1)}, u32[]{:S(2)}, u32[]{:S(2)}) collective-permute-start(bf16[2,4,160,128]{3,2,1,0:T(8,128)(2,1)S(1)} %get-tuple-element.29), channel_id=1, source_target_pairs={{0,32},{32,64},{64,96},{96,128},{128,160},{160,192},{192,224},{224... | collective-permute-start | bytes 983048 | tf_op jit(solution)/shard_map/ppermute | solution.py:321
  26.0 9.6 %collective-permute-start.2 = (bf16[2,4,160,128]{3,2,1,0:T(8,128)(2,1)S(1)}, bf16[2,4,160,128]{3,2,1,0:T(8,128)(2,1)S(1)}, u32[]{:S(2)}, u32[]{:S(2)}) collective-permute-start(bf16[2,4,160,128]{3,2,1,0:T(8,128)(2,1)S(1)} %get-tuple-element.30), channel_id=1, source_target_pairs={{0,224},{32,0},{64,32},{96,64},{128,96},{160,128},{192,160},{224,1... | collective-permute-start | bytes 983048 | tf_op jit(solution)/shard_map/ppermute | solution.py:321
  35.7 43.7 %copy-start.10 = (s32[1,8]{1,0:T(1,128)S(1)}, s32[1,8]{1,0:T(1,128)}, u32[]{:S(2)}) copy-start(s32[1,8]{1,0:T(1,128)} %flags_ref.1) | copy-start | bytes 100
  35.7 58.5 %copy-start.1 = (bf16[256,1024]{1,0:T(8,128)(2,1)S(1)}, bf16[256,1024]{1,0:T(8,128)(2,1)}, u32[]{:S(2)}) copy-start(bf16[256,1024]{1,0:T(8,128)(2,1)} %g_hbm.3) | copy-start | bytes 1572868
  35.7 58.5 %copy-start.2 = (bf16[256,128]{1,0:T(8,128)(2,1)S(1)}, bf16[256,128]{1,0:T(8,128)(2,1)}, u32[]{:S(2)}) copy-start(bf16[256,128]{1,0:T(8,128)(2,1)} %get-tuple-element.35.back_hbm) | copy-start | bytes 196612
  80.7 23.3 %all-to-all-start.2 = ((f32[256,1,128]{2,1,0:T(1,128)}), f32[256,1,128]{2,1,0:T(1,128)S(1)}, u32[]{:S(2)}, u32[]{:S(2)}) async-start(f32[256,1,128]{2,1,0:T(1,128)} %get-tuple-element.33), calls=%async_computation.2 | async-start | bytes 262144 | tf_op jit(solution)/shard_map/all_to_all | solution.py:390
  94.2 9.8 %copy-start.4 = (f32[32,128]{1,0:T(8,128)S(1)}, f32[32,128]{1,0:T(8,128)}, u32[]{:S(2)}) copy-start(f32[32,128]{1,0:T(8,128)} %master_a.1) | copy-start | bytes 49156
  94.2 9.8 %copy-start.5 = (f32[32,128]{1,0:T(8,128)S(1)}, f32[32,128]{1,0:T(8,128)}, u32[]{:S(2)}) copy-start(f32[32,128]{1,0:T(8,128)} %moment_a.1) | copy-start | bytes 49156
  94.2 9.8 %copy-start.6 = (f32[32,128]{1,0:T(8,128)S(1)}, f32[32,128]{1,0:T(8,128)}, u32[]{:S(2)}) copy-start(f32[32,128]{1,0:T(8,128)} %second_a.1) | copy-start | bytes 49156
  94.2 9.8 %copy-start.7 = (f32[4,128]{1,0:T(4,128)S(1)}, f32[4,128]{1,0:T(4,128)}, u32[]{:S(2)}) copy-start(f32[4,128]{1,0:T(4,128)} %master_b.1) | copy-start | bytes 6148
  94.2 9.8 %copy-start.8 = (f32[4,128]{1,0:T(4,128)S(1)}, f32[4,128]{1,0:T(4,128)}, u32[]{:S(2)}) copy-start(f32[4,128]{1,0:T(4,128)} %moment_b.1) | copy-start | bytes 6148
  94.2 9.8 %copy-start.9 = (f32[4,128]{1,0:T(4,128)S(1)}, f32[4,128]{1,0:T(4,128)}, u32[]{:S(2)}) copy-start(f32[4,128]{1,0:T(4,128)} %second_b.1) | copy-start | bytes 6148
Sparse Core Ops, SparseCore 0:
  10.6 83.6 all-gather.1
